TPU v7x, 32 devices: a whole 2x2x4 slice. The times are simulated.
32 devices in a mesh: visit: 8 (over y, x, core), sky: 4 (over z).
Axes of the slice: x: 2, y: 2, z: 4, core: 2. Of those that a mesh axis runs over, the one named last changes fastest.
Arguments:
- image: bfloat16 [8, 384, 2048], P('visit', None, 'sky'), may hold values from -16 to 16
- variance: bfloat16 [8, 384, 2048], P('visit', None, 'sky'), may hold values from 0.25 to 4
- mask_bits: int32 [8, 384, 2048], P('visit', None, 'sky'), may hold values from 0 to 63, as said below
- boxes: int32 [8, 4], P('visit'), may hold values from 0 to 2048, as said below
- row_filters: bfloat16 [20, 41], replicated, may hold values from -1 to 1
- col_filters: bfloat16 [20, 41], replicated, may hold values from -1 to 1
- coeffs: float32 [8, 20, 6], P('visit'), may hold values from -1.25 to 1.25
Outputs:
- coadd: float32 [384, 2048], P('visit', 'sky')
- weight_sum: float32 [384, 2048], P('visit', 'sky')
Inputs may be any that keep to these rules, and one draw needn't show every extreme that they name: `mask_bits`: bits 0 to 5 may be set; bits 0, 1 and 2 reject a pixel. `boxes`: for every piece the first row is below the end row and the first column below the end column.
All inputs are finite; a program needn't handle non-finite values.
Results may differ from a plain program's by a relative error of at most 0.0029.
Values may be sent and summed in bfloat16 or wider, within the bound.
A program may use at most 64 MiB of HBM per device.

v0:
```python
import functools

import jax
import jax.numpy as jnp
from jax import lax
from jax.experimental import pallas as pl
from jax.experimental.pallas import tpu as pltpu
from jax.sharding import PartitionSpec as P

RAD = 20
ROWS_DEV = 48
REJECT = 7
LANES = 128
GROUP = 4
BAND = GROUP * ROWS_DEV
PAD = 32
WIN = BAND + 2 * PAD
UNITS = 2
MESH = pl.DeviceIdType.MESH


def kernel(
    visits,
    skies,
    image_hbm,
    var_hbm,
    bits_hbm,
    boxes_hbm,
    rowf_hbm,
    colf_hbm,
    coef_hbm,
    sums_ref,
    image_ref,
    var_ref,
    bits_ref,
    boxes_ref,
    rowf_ref,
    colf_ref,
    coef_ref,
    halo_l,
    halo_r,
    masked,
    got_var,
    matched,
    got_pix,
    total,
    windows,
    row_mats,
    col_mats,
    pass_a,
    pass_b,
    filt,
    load_sem,
    var_send,
    var_recv,
    pix_send,
    pix_recv,
    halo_send,
    halo_recv,
):
    height, cols = image_ref.shape[1], image_ref.shape[2]
    width = cols * skies
    basis, taps = rowf_ref.shape
    blocks = cols // LANES
    per_unit = blocks // UNITS
    span = per_unit * LANES
    order = list(range(1, blocks - 1)) + [0, blocks - 1]
    groups = visits // GROUP
    few = visits <= 8
    v = lax.axis_index("visit")
    z = lax.axis_index("sky")
    my_group = v // GROUP
    has_l = z > 0
    has_r = z < skies - 1

    barrier = pltpu.get_barrier_semaphore()
    for step in range(1, visits):
        pl.semaphore_signal(
            barrier, inc=1, device_id=(lax.rem(v + step, visits), z), device_id_type=MESH
        )

    @pl.when(has_l)
    def _():
        pl.semaphore_signal(barrier, inc=1, device_id=(v, z - 1), device_id_type=MESH)

    @pl.when(has_r)
    def _():
        pl.semaphore_signal(barrier, inc=1, device_id=(v, z + 1), device_id_type=MESH)

    pairs = (
        (boxes_hbm, boxes_ref),
        (var_hbm, var_ref),
        (bits_hbm, bits_ref),
        (rowf_hbm, rowf_ref),
        (colf_hbm, colf_ref),
        (image_hbm, image_ref),
        (coef_hbm, coef_ref),
    )
    loads = [
        pltpu.make_async_copy(src, dst, load_sem.at[n]) for n, (src, dst) in enumerate(pairs)
    ]
    for load in loads:
        load.start()

    for load in loads[:3]:
        load.wait()
    col_first = z * cols
    box = [boxes_ref[0, i] for i in range(4)]
    col_index = col_first + lax.broadcasted_iota(jnp.int32, (ROWS_DEV, cols), 1)
    col_inside = (col_index >= box[2]) & (col_index < box[3])
    row_iota = lax.broadcasted_iota(jnp.int32, (ROWS_DEV, cols), 0)

    def mask_band(band, carry):
        first = pl.multiple_of(band * ROWS_DEV, ROWS_DEV)
        rows = pl.ds(first, ROWS_DEV)
        row_index = first + row_iota
        inside = (row_index >= box[0]) & (row_index < box[1]) & col_inside
        inside = inside & ((bits_ref[0, rows, :] & REJECT) == 0)
        masked[rows, :] = jnp.where(inside, var_ref[0, rows, :].astype(jnp.float32), 0.0).astype(
            jnp.bfloat16
        )
        return carry

    lax.fori_loop(0, visits, mask_band, 0, unroll=few)

    pl.semaphore_wait(barrier, visits - 1 + has_l.astype(jnp.int32) + has_r.astype(jnp.int32))

    def halo_copy(first, dst, send, recv, target):
        return pltpu.make_async_remote_copy(
            src_ref=image_hbm.at[0, :, pl.ds(first, LANES)],
            dst_ref=dst,
            send_sem=halo_send.at[send],
            recv_sem=halo_recv.at[recv],
            device_id=(v, target),
            device_id_type=MESH,
        )

    @pl.when(has_l)
    def _():
        halo_copy(0, halo_r, 0, 1, z - 1).start()

    @pl.when(has_r)
    def _():
        halo_copy(cols - LANES, halo_l, 1, 0, z + 1).start()

    def rows_of(dest):
        return pl.ds(pl.multiple_of(dest * ROWS_DEV, ROWS_DEV), ROWS_DEV)

    def var_copy(dest, source):
        return pltpu.make_async_remote_copy(
            src_ref=masked.at[rows_of(dest), :],
            dst_ref=got_var.at[source],
            send_sem=var_send.at[dest],
            recv_sem=var_recv.at[source],
            device_id=(dest, z),
            device_id_type=MESH,
        )

    def pix_copy(unit, dest, source):
        return pltpu.make_async_remote_copy(
            src_ref=matched.at[unit, rows_of(dest), :],
            dst_ref=got_pix.at[unit, source],
            send_sem=pix_send.at[unit, dest],
            recv_sem=pix_recv.at[unit, source],
            device_id=(dest, z),
            device_id_type=MESH,
        )

    for step in range(1, visits):
        dest = lax.rem(v + step, visits)
        var_copy(dest, v).start()

    filt[...] = jnp.zeros_like(filt)
    loads[3].wait()
    loads[4].wait()
    filt[0, 0:basis, 0:taps] = rowf_ref[...].astype(jnp.float32)
    filt[1, 0:basis, 0:taps] = colf_ref[...].astype(jnp.float32)
    filt[0] = pltpu.roll(filt[0], PAD - RAD, 1)

    def build(b):
        row = jnp.broadcast_to(filt[0, pl.ds(b, 1), :], (BAND, WIN))
        row_mats[b] = pltpu.roll(row, 0, 1, stride=1, stride_axis=0).astype(jnp.bfloat16)
        col = jnp.broadcast_to(filt[1, pl.ds(b, 1), :], (LANES, 2 * LANES))
        col_mats[b] = pltpu.roll(col, 0, 1, stride=1, stride_axis=0).astype(jnp.bfloat16)

    for k in range(blocks):
        windows[k, 0:PAD, :] = jnp.zeros((PAD, 2 * LANES), jnp.bfloat16)
        windows[k, PAD + height : PAD + height + PAD, :] = jnp.zeros((PAD, 2 * LANES), jnp.bfloat16)

    def shifted(parts, lanes):
        wide = jnp.concatenate(parts, axis=1).astype(jnp.float32)
        back = wide.shape[1] - (LANES - RAD)
        return pltpu.roll(wide, back, 1)[:, :lanes].astype(jnp.bfloat16)

    def window_rows(first):
        return pl.ds(pl.multiple_of(first + PAD, 16), ROWS_DEV)

    def inner_band(band, carry):
        first = pl.multiple_of(band * ROWS_DEV, ROWS_DEV)
        wide = shifted([image_ref[0, pl.ds(first, ROWS_DEV), :]], cols - LANES)
        for k in range(blocks - 2):
            windows[k, window_rows(first), :] = wide[:, k * LANES : (k + 2) * LANES]
        return carry

    def outer_band(band, carry):
        first = pl.multiple_of(band * ROWS_DEV, ROWS_DEV)
        rows = pl.ds(first, ROWS_DEV)
        left = shifted([halo_l[rows, :], image_ref[0, rows, 0 : 2 * LANES]], 2 * LANES)
        windows[blocks - 2, window_rows(first), :] = left
        right = shifted([image_ref[0, rows, cols - 2 * LANES : cols], halo_r[rows, :]], 2 * LANES)
        windows[blocks - 1, window_rows(first), :] = right
        return carry

    loads[5].wait()
    loads[6].wait()
    lax.fori_loop(0, visits, inner_band, 0, unroll=few)

    lane = lax.broadcasted_iota(jnp.int32, (1, LANES), 1)
    y_iota = lax.broadcasted_iota(jnp.int32, (BAND, LANES), 0)

    def one_unit(unit, group, prepare=False):
        first = pl.multiple_of(group * BAND, BAND)
        yc = (2.0 * (first + y_iota).astype(jnp.float32) + 1.0) / height - 1.0
        mine = order[unit * per_unit : (unit + 1) * per_unit]
        xs = []
        for k in mine:
            col_pos = (col_first + k * LANES + lane).astype(jnp.float32)
            xs.append((2.0 * col_pos + 1.0) / width - 1.0)

        def col_step(p, passed):
            image_win = windows[unit * per_unit : (unit + 1) * per_unit, pl.ds(first, WIN), :]
            mats = col_mats[pl.ds(2 * p, 2)].reshape(2 * LANES, 2 * LANES)
            out = lax.dot_general(
                image_win.reshape(per_unit * WIN, 2 * LANES),
                mats,
                (((1,), (1,)), ((), ())),
                preferred_element_type=jnp.float32,
            ).astype(jnp.bfloat16)
            for k in range(per_unit):
                for h in range(2):
                    passed[h, :, k * LANES : (k + 1) * LANES] = out[
                        k * WIN : (k + 1) * WIN, h * LANES : (h + 1) * LANES
                    ]

        def row_step(p, passed):
            parts = []
            for h in range(2):
                b = 2 * p + h
                rowpass = jnp.dot(row_mats[b], passed[h], preferred_element_type=jnp.float32)
                parts.append((rowpass, [coef_ref[t, 0, b] for t in range(6)]))
            for k in range(per_unit):
                lanes = slice(k * LANES, (k + 1) * LANES)
                add = 0.0 if p == 0 else total[unit, :, lanes]
                for rowpass, c in parts:
                    in_x = c[0] + c[1] * xs[k] + c[3] * (xs[k] * xs[k])
                    field = in_x + yc * ((c[2] + c[4] * xs[k]) + c[5] * yc)
                    add = add + field * rowpass[:, lanes]
                total[unit, :, lanes] = add

        buffers = (pass_a, pass_b)
        last = basis // 2 - 1
        if prepare:
            build(0)
            build(1)
        col_step(0, buffers[0])
        for p in range(last + 1):
            if prepare and p < last:
                build(2 * p + 2)
                build(2 * p + 3)
            if p < last:
                col_step(p + 1, buffers[(p + 1) % 2])
            row_step(p, buffers[p % 2])
        matched[unit, pl.ds(first, BAND), :] = total[unit].astype(jnp.bfloat16)
        for j in range(GROUP):
            dest = group * GROUP + j

            @pl.when(dest != v)
            def _():
                pix_copy(unit, dest, v).start()

    def group_at(step):
        return lax.rem(my_group + 1 + step, groups)

    one_unit(0, group_at(0), True)

    @pl.when(has_l)
    def _():
        halo_copy(0, halo_l, 0, 0, z - 1).wait_recv()

    @pl.when(has_r)
    def _():
        halo_copy(0, halo_r, 1, 1, z + 1).wait_recv()

    @pl.when(jnp.logical_not(has_l))
    def _():
        halo_l[...] = jnp.zeros_like(halo_l)

    @pl.when(jnp.logical_not(has_r))
    def _():
        halo_r[...] = jnp.zeros_like(halo_r)

    lax.fori_loop(0, visits, outer_band, 0, unroll=few)
    one_unit(1, group_at(0))

    def one_group(step, carry):
        for unit in range(UNITS):
            one_unit(unit, group_at(step))
        return carry

    lax.fori_loop(1, groups, one_group, 0)

    def weight_of(plane):
        plane = plane.astype(jnp.float32)
        positive = plane > 0
        return jnp.where(positive, 1.0 / jnp.where(positive, plane, 1.0), 0.0)

    own_first = pl.multiple_of((v - my_group * GROUP) * ROWS_DEV, ROWS_DEV)
    own_weight = weight_of(masked[rows_of(v), :])
    sums_ref[1] = own_weight

    def in_order(plane_of):
        lanes_of = {}
        for n, k in enumerate(order):
            part = plane_of(n // per_unit)
            at = n % per_unit * LANES
            lanes_of[k] = part[:, at : at + LANES]
        return jnp.concatenate([lanes_of[k] for k in range(blocks)], axis=1)

    sums_ref[0] = own_weight * in_order(lambda unit: total[unit, pl.ds(own_first, ROWS_DEV), :])

    def add_weight(step, carry):
        source = lax.rem(v + step, visits)
        var_copy(source, source).wait_recv()
        sums_ref[1] += weight_of(got_var[source])
        return carry

    lax.fori_loop(1, visits, add_weight, 0, unroll=few)

    base = my_group * GROUP

    def add_source(source):
        for unit in range(UNITS):
            pix_copy(unit, source, source).wait_recv()
        pixels = in_order(lambda unit: got_pix[unit, source]).astype(jnp.float32)
        sums_ref[0] += weight_of(got_var[source]) * pixels

    def add_far(step, carry):
        add_source(lax.rem(base + GROUP + step, visits))
        return carry

    def add_near(step, carry):
        add_source(base + lax.rem(v - base + step, GROUP))
        return carry

    lax.fori_loop(0, visits - GROUP, add_far, 0, unroll=few)
    lax.fori_loop(1, GROUP, add_near, 0, unroll=few)

    for step in range(1, visits):
        dest = lax.rem(v + step, visits)
        var_copy(dest, v).wait_send()
        for unit in range(UNITS):
            pix_copy(unit, dest, v).wait_send()

    @pl.when(has_l)
    def _():
        halo_copy(0, halo_r, 0, 1, z - 1).wait_send()

    @pl.when(has_r)
    def _():
        halo_copy(cols - LANES, halo_l, 1, 0, z + 1).wait_send()


def per_device(image, variance, mask_bits, boxes, row_filters, col_filters, coeffs):
    height, cols = image.shape[1], image.shape[2]
    visits, skies = lax.axis_size("visit"), lax.axis_size("sky")
    basis = row_filters.shape[0]
    blocks = cols // LANES
    span = cols // UNITS
    coeffs = jnp.transpose(coeffs, (2, 0, 1))
    hbm = pl.BlockSpec(memory_space=pltpu.HBM)
    f32, bf16 = jnp.float32, jnp.bfloat16
    dma = pltpu.SemaphoreType.DMA
    sums = pl.pallas_call(
        functools.partial(kernel, visits, skies),
        out_shape=jax.ShapeDtypeStruct((2, ROWS_DEV, cols), f32),
        in_specs=[hbm] * 7,
        out_specs=pl.BlockSpec(memory_space=pltpu.VMEM),
        scratch_shapes=[
            pltpu.VMEM(image.shape, bf16),
            pltpu.VMEM(variance.shape, bf16),
            pltpu.VMEM(mask_bits.shape, jnp.int32),
            pltpu.SMEM(boxes.shape, jnp.int32),
            pltpu.VMEM(row_filters.shape, bf16),
            pltpu.VMEM(col_filters.shape, bf16),
            pltpu.SMEM(coeffs.shape, f32),
            pltpu.VMEM((height, LANES), bf16),
            pltpu.VMEM((height, LANES), bf16),
            pltpu.VMEM((height, cols), bf16),
            pltpu.VMEM((visits, ROWS_DEV, cols), bf16),
            pltpu.VMEM((UNITS, height, span), bf16),
            pltpu.VMEM((UNITS, visits, ROWS_DEV, span), bf16),
            pltpu.VMEM((UNITS, BAND, span), f32),
            pltpu.VMEM((blocks, height + 2 * PAD, 2 * LANES), bf16),
            pltpu.VMEM((basis, BAND, WIN), bf16),
            pltpu.VMEM((basis, LANES, 2 * LANES), bf16),
            pltpu.VMEM((2, WIN, span), bf16),
            pltpu.VMEM((2, WIN, span), bf16),
            pltpu.VMEM((2, 24, WIN), f32),
            dma((7,)),
            dma((visits,)),
            dma((visits,)),
            dma((UNITS, visits)),
            dma((UNITS, visits)),
            dma((2,)),
            dma((2,)),
        ],
        compiler_params=pltpu.CompilerParams(
            collective_id=0, has_side_effects=True, vmem_limit_bytes=62 * 1024 * 1024
        ),
    )(image, variance, mask_bits, boxes, row_filters, col_filters, coeffs)
    return (sums[0] / jnp.maximum(sums[1], 1.0), sums[1])


def solution(mesh):
    in_specs = (
        P("visit", None, "sky"),
        P("visit", None, "sky"),
        P("visit", None, "sky"),
        P("visit", None),
        P(),
        P(),
        P("visit", None, None),
    )
    out_specs = (P("visit", "sky"), P("visit", "sky"))
    return jax.shard_map(
        per_device, mesh=mesh, in_specs=in_specs, out_specs=out_specs, check_vma=False
    )
```

profile of v0, /device:TPU:0, one launch (start us, length us, event | category | flops | bytes accessed | tf_op | source)
XLA Modules:
  0.0 22.4 jit_solution(12225519640197390253)
XLA Ops:
  0.6 20.1 %shard_map.86 = f32[2,48,512]{2,1,0:T(8,128)} custom-call(bf16[1,384,512]{2,1,0:T(8,128)(2,1)} %image_hbm.1, bf16[1,384,512]{2,1,0:T(8,128)(2,1)} %var_hbm.1, s32[1,384,512]{2,1,0:T(8,128)} %bits_hbm.1, s32[1,4]{1,0:T(1,128)} %boxes_hbm.1, bf16[20,41]{1,0:T(8,128)(2,1)} %rowf_hbm.1, bf16[20,41]{1,0:T(8,128)(2,1)} %colf_hbm.1, f32[6,1,20]{2,1,0:T(1,128)} %bitcast.6), custom_call_target="tpu_custom_call" | custom-call | tf_op jit(solution)/shard_map/pallas_call | solution.py:383
  20.8 1.6 %bitcast_divide_fusion = (f32[48,512]{1,0:T(8,128)}, f32[48,512]{1,0:T(8,128)}) fusion(f32[2,48,512]{2,1,0:T(8,128)} %shard_map.86), kind=kLoop, calls=%fused_computation | loop fusion | flops 49152 | bytes 393216 | tf_op jit(solution)/shard_map/div | solution.py:421
where the time goes:
time: 22.5 us; the launch traced here: 22.4 us
  Pallas kernels  20.1 us (89%)
  other arithmetic  1.62 us (7%)
  between operations  0.64 us (3%)
    pallas_call x1, Pallas kernels, per_device(): pl.pallas_call(functools.partial(kernel, visits, skies), out_shape=jax.Sh...  20.1 us
    div x1, other arithmetic, per_device(): return (sums[0] / jnp.maximum(sums[1], 1.0), sums[1])  1.62 us

commit v1 on v0

v1 whole, which is shorter than its diff:
```python
import functools

import jax
import jax.numpy as jnp
from jax import lax
from jax.experimental import pallas as pl
from jax.experimental.pallas import tpu as pltpu
from jax.sharding import PartitionSpec as P

RAD = 20
ROWS_DEV = 48
REJECT = 7
LANES = 128
CORES = 2
LEAD = 8
TOP = 24
WIN = 2 * ROWS_DEV
PACK = 5
TERMS = 6
MESH = pl.DeviceIdType.MESH


def weight_of(plane):
    plane = plane.astype(jnp.float32)
    positive = plane > 0
    return jnp.where(positive, 1.0 / jnp.where(positive, plane, 1.0), 0.0)


def kernel(
    visits,
    skies,
    image_hbm,
    var_hbm,
    bits_hbm,
    boxes_hbm,
    rowf_hbm,
    colf_hbm,
    coef_hbm,
    sums_ref,
    image_ref,
    var_ref,
    bits_ref,
    boxes_ref,
    rowf_ref,
    colf_ref,
    coef_ref,
    edge_send,
    edge_got,
    wide,
    masked,
    sib_var,
    pair_w,
    got_w,
    own_pix,
    sib_send,
    sib_pix,
    pair_pix,
    got_pix,
    filt,
    col_mats,
    passed,
    toeplitz,
    factors,
    row_mats,
    row_last,
    load_sem,
    halo_send,
    halo_recv,
    var_send,
    var_recv,
    w_send,
    w_recv,
    sib_send_sem,
    sib_recv_sem,
    pix_send,
    pix_recv,
):
    height, cols = var_ref.shape[1], var_ref.shape[2]
    width = cols * skies
    basis, taps = rowf_ref.shape
    blocks = cols // LANES
    inner, outer = list(range(1, blocks - 1)), [0, blocks - 1]
    chips = visits // CORES
    few = chips == 4
    deep = basis * WIN
    f32, bf16 = jnp.float32, jnp.bfloat16
    v = lax.axis_index("visit")
    z = lax.axis_index("sky")
    chip = v // CORES
    core = lax.rem(v, CORES)
    sibling = chip * CORES + 1 - core
    has_l = z > 0
    has_r = z < skies - 1

    def chip_at(slot):
        if not few:
            return lax.rem(chip + slot + 1, chips)
        return [chips - 1 - chip, lax.rem(chip + 2, chips), chip + 1 - 2 * lax.rem(chip, 2), chip][slot]

    def each(first, last, body):
        if few:
            for slot in range(first, last):
                body(slot)
        else:

            def one(slot, carry):
                body(slot)
                return carry

            lax.fori_loop(first, last, one, 0)

    barrier = pltpu.get_barrier_semaphore()
    pl.semaphore_signal(barrier, inc=1, device_id=(sibling, z), device_id_type=MESH)
    for slot in range(chips - 1):
        pl.semaphore_signal(
            barrier, inc=1, device_id=(chip_at(slot) * CORES + core, z), device_id_type=MESH
        )

    @pl.when(has_l)
    def _():
        pl.semaphore_signal(barrier, inc=1, device_id=(v, z - 1), device_id_type=MESH)

    @pl.when(has_r)
    def _():
        pl.semaphore_signal(barrier, inc=1, device_id=(v, z + 1), device_id_type=MESH)

    pairs = (
        (image_hbm.at[0], image_ref.at[pl.ds(16, height)]),
        (rowf_hbm, rowf_ref),
        (colf_hbm, colf_ref),
        (coef_hbm, coef_ref),
        (boxes_hbm, boxes_ref),
        (var_hbm, var_ref),
        (bits_hbm, bits_ref),
    )
    loads = [
        pltpu.make_async_copy(src, dst, load_sem.at[n]) for n, (src, dst) in enumerate(pairs)
    ]
    for load in loads:
        load.start()

    below = image_ref.shape[0] - 16 - height
    image_ref[0:16, :] = jnp.zeros((16, cols), bf16)
    image_ref[16 + height :, :] = jnp.zeros((below, cols), bf16)
    for b in range(basis):
        passed[b, 0:16, :] = jnp.zeros((16, cols), bf16)
        passed[b, height + 32 : height + 48, :] = jnp.zeros((16, cols), bf16)

    for load in loads[1:4]:
        load.wait()
    filt[...] = jnp.zeros_like(filt)
    filt[0:basis, 0:taps] = colf_ref[...].astype(f32)

    def build(b):
        col = jnp.broadcast_to(filt[pl.ds(b, 1), :], (LANES, 2 * LANES))
        col_mats[b] = pltpu.roll(col, 0, 1, stride=1, stride_axis=0).astype(bf16)

    col_first = z * cols
    group_of = lax.broadcasted_iota(jnp.int32, (1, deep), 1) // WIN
    tap_of = lax.broadcasted_iota(jnp.int32, (1, deep), 1) - group_of * WIN - (TOP - RAD)
    tap_mat = (lax.broadcasted_iota(jnp.int32, (taps, deep), 0) == tap_of).astype(f32).astype(bf16)
    own_group = (lax.broadcasted_iota(jnp.int32, (basis, deep), 0) == group_of).astype(f32)
    every = jnp.dot(rowf_ref[...], tap_mat, preferred_element_type=f32)
    line = jnp.sum(every * own_group, axis=0, keepdims=True)
    toeplitz[...] = pltpu.roll(
        jnp.broadcast_to(line, (ROWS_DEV, deep)), 0, 1, stride=1, stride_axis=0
    )
    c = jnp.dot(
        coef_ref[:, 0, :], own_group, precision=lax.Precision.HIGHEST, preferred_element_type=f32
    )
    c = [c[t : t + 1] for t in range(TERMS)]
    xc = (2 * col_first + cols).astype(f32) / width - 1.0
    factors[0:1] = c[0] + xc * (c[1] + xc * c[3])
    factors[1:2] = c[2] + xc * c[4]
    factors[2:3] = c[5]
    factors[3:4] = c[1] + (2.0 * xc) * c[3]
    factors[4:5] = c[4]
    row_last[...] = (toeplitz[...] * c[3]).astype(bf16)
    y_iota = lax.broadcasted_iota(jnp.int32, (ROWS_DEV, LANES), 0)
    tiles = deep // LANES

    def build_rows(band, at, first, last, tie):
        y = (2.0 * (band * ROWS_DEV + y_iota).astype(f32) + 1.0) / height - 1.0 + tie
        for n in range(first, last):
            lanes = slice(n * LANES, (n + 1) * LANES)
            base = toeplitz[:, lanes]
            f = [factors[t : t + 1, lanes] for t in range(5)]
            row_mats[at, 0:ROWS_DEV, lanes] = (base * (f[0] + y * (f[1] + y * f[2]))).astype(bf16)
            row_mats[at, ROWS_DEV : 2 * ROWS_DEV, lanes] = (base * (f[3] + y * f[4])).astype(bf16)

    lane = lax.broadcasted_iota(jnp.int32, (1, LANES), 1)
    strip = wide.shape[0] // PACK
    loads[0].wait()
    to_l = to_r = jnp.zeros((strip, LANES), f32)
    for g in range(PACK):
        rows = slice(g * strip, (g + 1) * strip)
        part = image_ref[g * strip : (g + 1) * strip + 16, :].astype(f32)[LEAD : LEAD + strip]
        part = pltpu.roll(part, RAD, 1)
        wide[rows, LANES:cols] = part[:, LANES:].astype(bf16)
        edge = part[:, :LANES]
        wide[rows, cols:] = edge.astype(bf16)
        at = g * RAD
        edge = pltpu.roll(edge, at, 1) if g else edge
        to_r = jnp.where((lane >= at) & (lane < at + RAD), edge, to_r)
        to_l = jnp.where((lane >= at + RAD) & (lane < at + 2 * RAD), edge, to_l)
    edge_send[0] = to_l.astype(bf16)
    edge_send[1] = to_r.astype(bf16)

    for load in loads[4:]:
        load.wait()
    box = [boxes_ref[0, i] for i in range(4)]
    col_index = col_first + lax.broadcasted_iota(jnp.int32, (ROWS_DEV, cols), 1)
    col_inside = (col_index >= box[2]) & (col_index < box[3])
    row_iota = lax.broadcasted_iota(jnp.int32, (ROWS_DEV, cols), 0)

    def mask_band(band, carry):
        first = pl.multiple_of(band * ROWS_DEV, ROWS_DEV)
        rows = pl.ds(first, ROWS_DEV)
        row_index = first + row_iota
        inside = (row_index >= box[0]) & (row_index < box[1]) & col_inside
        inside = inside & ((bits_ref[0, rows, :] & REJECT) == 0)
        masked[lax.rem(band, CORES), band // CORES] = jnp.where(
            inside, var_ref[0, rows, :].astype(f32), 0.0
        ).astype(bf16)
        return carry

    lax.fori_loop(0, visits, mask_band, 0, unroll=few)

    pl.semaphore_wait(barrier, chips + has_l.astype(jnp.int32) + has_r.astype(jnp.int32))

    def remote(src, dst, send, recv, target):
        return pltpu.make_async_remote_copy(
            src_ref=src,
            dst_ref=dst,
            send_sem=send,
            recv_sem=recv,
            device_id=target,
            device_id_type=MESH,
        )

    def edge_copy(side, target):
        return remote(
            edge_send.at[side],
            edge_got.at[side],
            halo_send.at[side],
            halo_recv.at[side],
            (v, target),
        )

    def peer(slot):
        return (chip_at(slot) * CORES + core, z)

    def var_copy():
        return remote(
            masked.at[1 - core], sib_var, var_send.at[0], var_recv.at[0], (sibling, z)
        )

    def w_copy(slot):
        return remote(
            pair_w.at[slot], got_w.at[slot], w_send.at[slot], w_recv.at[slot], peer(slot)
        )

    def sib_copy(slot):
        return remote(
            sib_send.at[slot],
            sib_pix.at[slot],
            sib_send_sem.at[slot],
            sib_recv_sem.at[slot],
            (sibling, z),
        )

    def pix_copy(slot):
        return remote(
            pair_pix.at[slot], got_pix.at[slot], pix_send.at[slot], pix_recv.at[slot], peer(slot)
        )

    @pl.when(has_l)
    def _():
        edge_copy(0, z - 1).start()

    @pl.when(has_r)
    def _():
        edge_copy(1, z + 1).start()

    var_copy().start()

    def col_step(p, first, rows, which):
        parts = [wide[pl.ds(first, rows), k * LANES : (k + 2) * LANES] for k in which]
        mats = col_mats[pl.ds(2 * p, 2)].reshape(2 * LANES, 2 * LANES)
        out = lax.dot_general(
            jnp.concatenate(parts, axis=0),
            mats,
            (((1,), (1,)), ((), ())),
            preferred_element_type=f32,
        )
        into = pl.ds(pl.multiple_of(first + 16, 16), rows)
        for n, k in enumerate(which):
            for h in range(2):
                passed[2 * p + h, into, k * LANES : (k + 1) * LANES] = out[
                    n * rows : (n + 1) * rows, h * LANES : (h + 1) * LANES
                ].astype(bf16)
        return out[0:1, 0:LANES] * 0.0

    def weighted(slot, side, at):
        at_chip = chip_at(slot)
        band = at_chip * CORES + side
        if not few:
            build_rows(band, at, 0, tiles, 0.0)
        rows = pl.ds(pl.multiple_of(band * ROWS_DEV, 16), WIN)
        mats = jnp.concatenate([row_mats[at], row_last[...]], axis=0)
        out = jnp.dot(mats, passed[:, rows, :].reshape(deep, cols), preferred_element_type=f32)
        x = (2 * lax.broadcasted_iota(jnp.int32, (1, cols), 1) + 1 - cols).astype(f32) / width
        pixels = out[0:ROWS_DEV] + x * (
            out[ROWS_DEV : 2 * ROWS_DEV] + x * out[2 * ROWS_DEV : 3 * ROWS_DEV]
        )
        return pixels * weight_of(masked[side, at_chip])

    def for_sibling(slot, at=0):
        sib_send[slot] = weighted(slot, 1 - core, at)

    def for_own(slot, at=0):
        own_pix[slot] = weighted(slot, core, at)

    def send_pair(slot):
        sib_copy(slot).wait_recv()
        pair_pix[slot] = (own_pix[slot] + sib_pix[slot]).astype(bf16)
        pix_copy(slot).start()

    def pair_weight(slot):
        at_chip = chip_at(slot)
        return weight_of(masked[core, at_chip]) + weight_of(sib_var[at_chip])

    def send_weight(slot):
        pair_w[slot] = pair_weight(slot).astype(bf16)
        w_copy(slot).start()

    def edges():
        @pl.when(has_l)
        def _():
            edge_copy(1, z - 1).wait_recv()

        @pl.when(has_r)
        def _():
            edge_copy(0, z + 1).wait_recv()

        @pl.when(jnp.logical_not(has_l))
        def _():
            edge_got[1] = jnp.zeros((strip, LANES), bf16)

        @pl.when(jnp.logical_not(has_r))
        def _():
            edge_got[0] = jnp.zeros((strip, LANES), bf16)

        for g in range(PACK):
            rows = slice(g * strip, (g + 1) * strip)
            mine = wide[rows, cols:].astype(f32)
            from_r, from_l = (edge_got[side].astype(f32) for side in range(2))
            if g:
                from_r = pltpu.roll(from_r, LANES - g * RAD, 1)
                from_l = pltpu.roll(from_l, LANES - g * RAD, 1)
            wide[rows, 0:LANES] = jnp.where(lane < RAD, from_l, mine).astype(bf16)
            wide[rows, cols:] = jnp.where(
                (lane >= RAD) & (lane < 2 * RAD), from_r, mine
            ).astype(bf16)

    def own_sums():
        sums_ref[1] = pair_weight(chips - 1)

    def add_weight(slot):
        w_copy(slot).wait_recv()
        sums_ref[1] += got_w[slot].astype(f32)

    def add_own():
        sib_copy(chips - 1).wait_recv()
        sums_ref[0] = own_pix[chips - 1] + sib_pix[chips - 1]

    def add_pixels(slot):
        pix_copy(slot).wait_recv()
        sums_ref[0] += got_pix[slot].astype(f32)

    steps = basis // 2
    if few:
        half = chips // 2 * CORES * ROWS_DEV
        group = chip // 2
        total = height + 2 * LEAD
        early = half + 2 * LEAD + LEAD * 2
        far = pl.multiple_of((1 - group) * (total - early), 16)
        near = pl.multiple_of(group * early, 16)
        bands = [(0, 1), (1, 1), (0, 0), (1, 0), (2, 1), (2, 0), (3, 1), (3, 0)]

        def band_of(at):
            slot, other = bands[at]
            return chip_at(slot) * CORES + (1 - core if other else core)

        def columns(first, rows, which, base, share, build_too=False):
            for p in range(steps):
                if build_too:
                    build(2 * p)
                    build(2 * p + 1)
                tie = col_step(p, first, rows, which)
                n = 3 * (p % share)
                build_rows(band_of(base + p // share), base + p // share, n, n + tiles // share, tie)

        share = 5
        columns(far, early, inner, 0, share, True)
        edges()
        var_copy().wait_recv()
        for slot in range(chips - 1):
            send_weight(slot)
        columns(far, early, outer, 2, share)
        for_sibling(0, 0)
        for_sibling(1, 1)
        sib_copy(0).start()
        sib_copy(1).start()
        for_own(0, 2)
        for_own(1, 3)
        columns(near, total - early, inner, 4, share)
        send_pair(0)
        send_pair(1)
        columns(near, total - early, outer, 6, share)
        for_sibling(2, 4)
        sib_copy(2).start()
        for_own(2, 5)
        for_sibling(3, 6)
        sib_copy(3).start()
        own_sums()
        for slot in range(chips - 1):
            add_weight(slot)
        for_own(3, 7)
        send_pair(2)
    else:
        edges()

        def one(p, carry):
            build(2 * p)
            build(2 * p + 1)
            for k in range(blocks):
                col_step(p, 0, height + 2 * LEAD, [k])
            return carry

        lax.fori_loop(0, steps, one, 0)
        var_copy().wait_recv()
        each(0, chips - 1, send_weight)

        def sibling_band(slot):
            for_sibling(slot)
            sib_copy(slot).start()

        each(0, chips, sibling_band)
        each(0, chips, for_own)
        each(0, chips - 1, send_pair)
        own_sums()
        each(0, chips - 1, add_weight)

    add_own()
    each(0, chips - 1, add_pixels)

    var_copy().wait_send()

    def drain(slot):
        w_copy(slot).wait_send()
        pix_copy(slot).wait_send()

    each(0, chips - 1, drain)
    each(0, chips, lambda slot: sib_copy(slot).wait_send())

    @pl.when(has_l)
    def _():
        edge_copy(0, z - 1).wait_send()

    @pl.when(has_r)
    def _():
        edge_copy(1, z + 1).wait_send()


def per_device(image, variance, mask_bits, boxes, row_filters, col_filters, coeffs):
    height, cols = image.shape[1], image.shape[2]
    visits, skies = lax.axis_size("visit"), lax.axis_size("sky")
    basis = row_filters.shape[0]
    chips = visits // CORES
    few = chips == 4
    deep = basis * WIN
    unit = 16 * PACK
    tall = (height + 2 * LEAD + unit - 1) // unit * unit
    coeffs = jnp.transpose(coeffs, (2, 0, 1))
    hbm = pl.BlockSpec(memory_space=pltpu.HBM)
    f32, bf16 = jnp.float32, jnp.bfloat16
    dma = pltpu.SemaphoreType.DMA
    sums = pl.pallas_call(
        functools.partial(kernel, visits, skies),
        out_shape=jax.ShapeDtypeStruct((2, ROWS_DEV, cols), f32),
        in_specs=[hbm] * 7,
        out_specs=pl.BlockSpec(memory_space=pltpu.VMEM),
        scratch_shapes=[
            pltpu.VMEM((tall + 16, cols), bf16),
            pltpu.VMEM(variance.shape, bf16),
            pltpu.VMEM(mask_bits.shape, jnp.int32),
            pltpu.SMEM(boxes.shape, jnp.int32),
            pltpu.VMEM(row_filters.shape, bf16),
            pltpu.VMEM(col_filters.shape, bf16),
            pltpu.VMEM(coeffs.shape, f32),
            pltpu.VMEM((2, tall // PACK, LANES), bf16),
            pltpu.VMEM((2, tall // PACK, LANES), bf16),
            pltpu.VMEM((tall, cols + LANES), bf16),
            pltpu.VMEM((CORES, chips, ROWS_DEV, cols), bf16),
            pltpu.VMEM((chips, ROWS_DEV, cols), bf16),
            pltpu.VMEM((chips, ROWS_DEV, cols), bf16),
            pltpu.VMEM((chips, ROWS_DEV, cols), bf16),
            pltpu.VMEM((chips, ROWS_DEV, cols), f32),
            pltpu.VMEM((chips, ROWS_DEV, cols), f32),
            pltpu.VMEM((chips, ROWS_DEV, cols), f32),
            pltpu.VMEM((chips, ROWS_DEV, cols), bf16),
            pltpu.VMEM((chips, ROWS_DEV, cols), bf16),
            pltpu.VMEM((24, 2 * LANES), f32),
            pltpu.VMEM((basis, LANES, 2 * LANES), bf16),
            pltpu.VMEM((basis, height + 2 * TOP, cols), bf16),
            pltpu.VMEM((ROWS_DEV, deep), f32),
            pltpu.VMEM((8, deep), f32),
            pltpu.VMEM((visits if few else 1, 2 * ROWS_DEV, deep), bf16),
            pltpu.VMEM((ROWS_DEV, deep), bf16),
            dma((7,)),
            dma((2,)),
            dma((2,)),
            dma((1,)),
            dma((1,)),
            dma((chips,)),
            dma((chips,)),
            dma((chips,)),
            dma((chips,)),
            dma((chips,)),
            dma((chips,)),
        ],
        compiler_params=pltpu.CompilerParams(
            collective_id=0, has_side_effects=True, vmem_limit_bytes=62 * 1024 * 1024
        ),
    )(image, variance, mask_bits, boxes, row_filters, col_filters, coeffs)
    return (sums[0] / jnp.maximum(sums[1], 1.0), sums[1])


def solution(mesh):
    in_specs = (
        P("visit", None, "sky"),
        P("visit", None, "sky"),
        P("visit", None, "sky"),
        P("visit", None),
        P(),
        P(),
        P("visit", None, None),
    )
    out_specs = (P("visit", "sky"), P("visit", "sky"))
    return jax.shard_map(
        per_device, mesh=mesh, in_specs=in_specs, out_specs=out_specs, check_vma=False
    )
```

time: 22.5 us -> 20 us (0.89)
  Pallas kernels: 20.1 us -> 17.6 us
    pallas_call x1, Pallas kernels: 20.1 us -> 17.6 us  [per_device(): pl.pallas_call(functools.partial(kernel, visits, skies), out_shape=jax.Sh...]
where the time goes in v1:
time: 20 us; the launch traced here: 19.9 us
  Pallas kernels  17.6 us (88%)
  other arithmetic  1.62 us (8%)
  between operations  0.64 us (3%)
    pallas_call x1, Pallas kernels, per_device(): pl.pallas_call(functools.partial(kernel, visits, skies), out_shape=jax.Sh...  17.6 us
    div x1, other arithmetic, per_device(): return (sums[0] / jnp.maximum(sums[1], 1.0), sums[1])  1.62 us

profile of v1, /device:TPU:0, one launch (start us, length us, event | category | flops | bytes accessed | tf_op | source)
XLA Modules:
  0.0 19.9 jit_solution(9633091694963706)
XLA Ops:
  0.6 17.6 %shard_map.86 = f32[2,48,512]{2,1,0:T(8,128)} custom-call(bf16[1,384,512]{2,1,0:T(8,128)(2,1)} %image_hbm.1, bf16[1,384,512]{2,1,0:T(8,128)(2,1)} %var_hbm.1, s32[1,384,512]{2,1,0:T(8,128)} %bits_hbm.1, s32[1,4]{1,0:T(1,128)} %boxes_hbm.1, bf16[20,41]{1,0:T(8,128)(2,1)} %rowf_hbm.1, bf16[20,41]{1,0:T(8,128)(2,1)} %colf_hbm.1, f32[6,1,20]{2,1,0:T(1,128)} %bitcast.6), custom_call_target="tpu_custom_call" | custom-call | tf_op jit(solution)/shard_map/pallas_call | solution.py:489
  18.2 1.6 %bitcast_divide_fusion = (f32[48,512]{1,0:T(8,128)}, f32[48,512]{1,0:T(8,128)}) fusion(f32[2,48,512]{2,1,0:T(8,128)} %shard_map.86), kind=kLoop, calls=%fused_computation | loop fusion | flops 49152 | bytes 393216 | tf_op jit(solution)/shard_map/div | solution.py:537

commit v2 on v1

--- a/solution.py
+++ b/solution.py
@@ -48,9 +48,7 @@
     edge_got,
     wide,
     masked,
-    sib_var,
-    pair_w,
-    got_w,
+    got_var,
     own_pix,
     sib_send,
     sib_pix,
@@ -68,8 +66,6 @@
     halo_recv,
     var_send,
     var_recv,
-    w_send,
-    w_recv,
     sib_send_sem,
     sib_recv_sem,
     pix_send,
@@ -110,10 +106,9 @@
             lax.fori_loop(first, last, one, 0)
 
     barrier = pltpu.get_barrier_semaphore()
-    pl.semaphore_signal(barrier, inc=1, device_id=(sibling, z), device_id_type=MESH)
-    for slot in range(chips - 1):
+    for step in range(1, visits):
         pl.semaphore_signal(
-            barrier, inc=1, device_id=(chip_at(slot) * CORES + core, z), device_id_type=MESH
+            barrier, inc=1, device_id=(lax.rem(v + step, visits), z), device_id_type=MESH
         )
 
     @pl.when(has_l)
@@ -125,10 +120,10 @@
         pl.semaphore_signal(barrier, inc=1, device_id=(v, z + 1), device_id_type=MESH)
 
     pairs = (
-        (image_hbm.at[0], image_ref.at[pl.ds(16, height)]),
         (rowf_hbm, rowf_ref),
         (colf_hbm, colf_ref),
         (coef_hbm, coef_ref),
+        (image_hbm.at[0], image_ref.at[pl.ds(16, height)]),
         (boxes_hbm, boxes_ref),
         (var_hbm, var_ref),
         (bits_hbm, bits_ref),
@@ -142,20 +137,27 @@
     below = image_ref.shape[0] - 16 - height
     image_ref[0:16, :] = jnp.zeros((16, cols), bf16)
     image_ref[16 + height :, :] = jnp.zeros((below, cols), bf16)
-    for b in range(basis):
-        passed[b, 0:16, :] = jnp.zeros((16, cols), bf16)
-        passed[b, height + 32 : height + 48, :] = jnp.zeros((16, cols), bf16)
-
-    for load in loads[1:4]:
+    col_first = z * cols
+    for pair in passed:
+        for h in range(2):
+            pair[h, 0:16, :] = jnp.zeros((16, cols), bf16)
+            pair[h, pair.shape[1] - 16 :, :] = jnp.zeros((16, cols), bf16)
+
+    for load in loads[:3]:
         load.wait()
     filt[...] = jnp.zeros_like(filt)
     filt[0:basis, 0:taps] = colf_ref[...].astype(f32)
+    lane = lax.broadcasted_iota(jnp.int32, (1, LANES), 1)
+    ahead = lax.broadcasted_iota(jnp.int32, (LANES, LANES), 1) >= lax.broadcasted_iota(
+        jnp.int32, (LANES, LANES), 0
+    )
 
     def build(b):
-        col = jnp.broadcast_to(filt[pl.ds(b, 1), :], (LANES, 2 * LANES))
-        col_mats[b] = pltpu.roll(col, 0, 1, stride=1, stride_axis=0).astype(bf16)
-
-    col_first = z * cols
+        col = jnp.broadcast_to(filt[pl.ds(b, 1), :], (LANES, LANES))
+        col = pltpu.roll(col, 0, 1, stride=1, stride_axis=0)
+        col_mats[b, :, 0:LANES] = jnp.where(ahead, col, 0.0).astype(bf16)
+        col_mats[b, :, LANES : 2 * LANES] = jnp.where(ahead, 0.0, col).astype(bf16)
+
     group_of = lax.broadcasted_iota(jnp.int32, (1, deep), 1) // WIN
     tap_of = lax.broadcasted_iota(jnp.int32, (1, deep), 1) - group_of * WIN - (TOP - RAD)
     tap_mat = (lax.broadcasted_iota(jnp.int32, (taps, deep), 0) == tap_of).astype(f32).astype(bf16)
@@ -185,12 +187,11 @@
             lanes = slice(n * LANES, (n + 1) * LANES)
             base = toeplitz[:, lanes]
             f = [factors[t : t + 1, lanes] for t in range(5)]
-            row_mats[at, 0:ROWS_DEV, lanes] = (base * (f[0] + y * (f[1] + y * f[2]))).astype(bf16)
-            row_mats[at, ROWS_DEV : 2 * ROWS_DEV, lanes] = (base * (f[3] + y * f[4])).astype(bf16)
-
-    lane = lax.broadcasted_iota(jnp.int32, (1, LANES), 1)
+            row_mats[at][0:ROWS_DEV, lanes] = (base * (f[0] + y * (f[1] + y * f[2]))).astype(bf16)
+            row_mats[at][ROWS_DEV : 2 * ROWS_DEV, lanes] = (base * (f[3] + y * f[4])).astype(bf16)
+
     strip = wide.shape[0] // PACK
-    loads[0].wait()
+    loads[3].wait()
     to_l = to_r = jnp.zeros((strip, LANES), f32)
     for g in range(PACK):
         rows = slice(g * strip, (g + 1) * strip)
@@ -206,6 +207,70 @@
     edge_send[0] = to_l.astype(bf16)
     edge_send[1] = to_r.astype(bf16)
 
+    def remote(src, dst, send, recv, target):
+        return pltpu.make_async_remote_copy(
+            src_ref=src,
+            dst_ref=dst,
+            send_sem=send,
+            recv_sem=recv,
+            device_id=target,
+            device_id_type=MESH,
+        )
+
+    def edge_copy(side, target):
+        return remote(
+            edge_send.at[side],
+            edge_got.at[side],
+            halo_send.at[side],
+            halo_recv.at[side],
+            (v, target),
+        )
+
+    def peer(slot):
+        return (chip_at(slot) * CORES + core, z)
+
+    def var_copy(slot, other):
+        side = 1 - core if other else core
+        return remote(
+            masked.at[side, chip_at(slot)],
+            got_var.at[slot, other],
+            var_send.at[slot, other],
+            var_recv.at[slot, other],
+            (chip_at(slot) * CORES + side, z),
+        )
+
+    def for_vars(act):
+        def both(slot):
+            act(slot, 0)
+            act(slot, 1)
+
+        each(0, chips - 1, both)
+        act(chips - 1, 1)
+
+    def sib_copy(slot):
+        return remote(
+            sib_send.at[slot],
+            sib_pix.at[slot],
+            sib_send_sem.at[slot],
+            sib_recv_sem.at[slot],
+            (sibling, z),
+        )
+
+    def pix_copy(slot):
+        return remote(
+            pair_pix.at[slot], got_pix.at[slot], pix_send.at[slot], pix_recv.at[slot], peer(slot)
+        )
+
+    pl.semaphore_wait(barrier, visits - 1 + has_l.astype(jnp.int32) + has_r.astype(jnp.int32))
+
+    @pl.when(has_l)
+    def _():
+        edge_copy(0, z - 1).start()
+
+    @pl.when(has_r)
+    def _():
+        edge_copy(1, z + 1).start()
+
     for load in loads[4:]:
         load.wait()
     box = [boxes_ref[0, i] for i in range(4)]
@@ -225,64 +290,7 @@
         return carry
 
     lax.fori_loop(0, visits, mask_band, 0, unroll=few)
-
-    pl.semaphore_wait(barrier, chips + has_l.astype(jnp.int32) + has_r.astype(jnp.int32))
-
-    def remote(src, dst, send, recv, target):
-        return pltpu.make_async_remote_copy(
-            src_ref=src,
-            dst_ref=dst,
-            send_sem=send,
-            recv_sem=recv,
-            device_id=target,
-            device_id_type=MESH,
-        )
-
-    def edge_copy(side, target):
-        return remote(
-            edge_send.at[side],
-            edge_got.at[side],
-            halo_send.at[side],
-            halo_recv.at[side],
-            (v, target),
-        )
-
-    def peer(slot):
-        return (chip_at(slot) * CORES + core, z)
-
-    def var_copy():
-        return remote(
-            masked.at[1 - core], sib_var, var_send.at[0], var_recv.at[0], (sibling, z)
-        )
-
-    def w_copy(slot):
-        return remote(
-            pair_w.at[slot], got_w.at[slot], w_send.at[slot], w_recv.at[slot], peer(slot)
-        )
-
-    def sib_copy(slot):
-        return remote(
-            sib_send.at[slot],
-            sib_pix.at[slot],
-            sib_send_sem.at[slot],
-            sib_recv_sem.at[slot],
-            (sibling, z),
-        )
-
-    def pix_copy(slot):
-        return remote(
-            pair_pix.at[slot], got_pix.at[slot], pix_send.at[slot], pix_recv.at[slot], peer(slot)
-        )
-
-    @pl.when(has_l)
-    def _():
-        edge_copy(0, z - 1).start()
-
-    @pl.when(has_r)
-    def _():
-        edge_copy(1, z + 1).start()
-
-    var_copy().start()
+    for_vars(lambda slot, other: var_copy(slot, other).start())
 
     def col_step(p, first, rows, which):
         parts = [wide[pl.ds(first, rows), k * LANES : (k + 2) * LANES] for k in which]
@@ -296,44 +304,63 @@
         into = pl.ds(pl.multiple_of(first + 16, 16), rows)
         for n, k in enumerate(which):
             for h in range(2):
-                passed[2 * p + h, into, k * LANES : (k + 1) * LANES] = out[
+                passed[p][h, into, k * LANES : (k + 1) * LANES] = out[
                     n * rows : (n + 1) * rows, h * LANES : (h + 1) * LANES
                 ].astype(bf16)
         return out[0:1, 0:LANES] * 0.0
 
-    def weighted(slot, side, at):
+    def picked(plane, which):
+        if len(which) == blocks:
+            return plane
+        return jnp.concatenate([plane[..., k * LANES : (k + 1) * LANES] for k in which], axis=-1)
+
+    def weighted(slot, side, at, which):
         at_chip = chip_at(slot)
         band = at_chip * CORES + side
         if not few:
             build_rows(band, at, 0, tiles, 0.0)
         rows = pl.ds(pl.multiple_of(band * ROWS_DEV, 16), WIN)
-        mats = jnp.concatenate([row_mats[at], row_last[...]], axis=0)
-        out = jnp.dot(mats, passed[:, rows, :].reshape(deep, cols), preferred_element_type=f32)
+        mats = jnp.concatenate([row_mats[at][...], row_last[...]], axis=0)
+        lines = jnp.concatenate(
+            [
+                jnp.concatenate(
+                    [
+                        pair[:, rows, k * LANES : (k + 1) * LANES].reshape(2 * WIN, LANES)
+                        for pair in passed
+                    ],
+                    axis=0,
+                )
+                for k in which
+            ],
+            axis=1,
+        )
+        out = jnp.dot(mats, lines, preferred_element_type=f32)
         x = (2 * lax.broadcasted_iota(jnp.int32, (1, cols), 1) + 1 - cols).astype(f32) / width
+        x = picked(x, which)
         pixels = out[0:ROWS_DEV] + x * (
             out[ROWS_DEV : 2 * ROWS_DEV] + x * out[2 * ROWS_DEV : 3 * ROWS_DEV]
         )
-        return pixels * weight_of(masked[side, at_chip])
-
-    def for_sibling(slot, at=0):
-        sib_send[slot] = weighted(slot, 1 - core, at)
-
-    def for_own(slot, at=0):
-        own_pix[slot] = weighted(slot, core, at)
+        return pixels * weight_of(picked(masked[side, at_chip], which)), out[0:1, 0:LANES] * 0.0
+
+    def put(ref, slot, side, at, which):
+        result, tie = weighted(slot, side, at, which)
+        for n, k in enumerate(which):
+            ref[slot, :, k * LANES : (k + 1) * LANES] = result[:, n * LANES : (n + 1) * LANES]
+        return tie
+
+    every_block = list(range(blocks))
+
+    def for_sibling(slot, at=0, which=every_block):
+        return put(sib_send, slot, 1 - core, at, which)
+
+    def for_own(slot, at=0, which=every_block):
+        return put(own_pix, slot, core, at, which)
 
     def send_pair(slot):
         sib_copy(slot).wait_recv()
         pair_pix[slot] = (own_pix[slot] + sib_pix[slot]).astype(bf16)
         pix_copy(slot).start()
 
-    def pair_weight(slot):
-        at_chip = chip_at(slot)
-        return weight_of(masked[core, at_chip]) + weight_of(sib_var[at_chip])
-
-    def send_weight(slot):
-        pair_w[slot] = pair_weight(slot).astype(bf16)
-        w_copy(slot).start()
-
     def edges():
         @pl.when(has_l)
         def _():
@@ -351,6 +378,7 @@
         def _():
             edge_got[0] = jnp.zeros((strip, LANES), bf16)
 
+    def merge_edges():
         for g in range(PACK):
             rows = slice(g * strip, (g + 1) * strip)
             mine = wide[rows, cols:].astype(f32)
@@ -363,12 +391,14 @@
                 (lane >= RAD) & (lane < 2 * RAD), from_r, mine
             ).astype(bf16)
 
-    def own_sums():
-        sums_ref[1] = pair_weight(chips - 1)
-
-    def add_weight(slot):
-        w_copy(slot).wait_recv()
-        sums_ref[1] += got_w[slot].astype(f32)
+    def add_weights():
+        sums_ref[1] = weight_of(masked[core, chip])
+
+        def one(slot, other):
+            var_copy(slot, other).wait_recv()
+            sums_ref[1] += weight_of(got_var[slot, other])
+
+        for_vars(one)
 
     def add_own():
         sib_copy(chips - 1).wait_recv()
@@ -392,55 +422,58 @@
             slot, other = bands[at]
             return chip_at(slot) * CORES + (1 - core if other else core)
 
-        def columns(first, rows, which, base, share, build_too=False):
+        def columns(first, rows, which, base, count, build_too=False):
+            pieces = [(base + n // tiles, n % tiles) for n in range(count * tiles)]
+            each_step = -(-len(pieces) // steps)
             for p in range(steps):
                 if build_too:
                     build(2 * p)
                     build(2 * p + 1)
                 tie = col_step(p, first, rows, which)
-                n = 3 * (p % share)
-                build_rows(band_of(base + p // share), base + p // share, n, n + tiles // share, tie)
-
-        share = 5
-        columns(far, early, inner, 0, share, True)
+                mine = pieces[p * each_step : (p + 1) * each_step]
+                for at in sorted({at for at, _ in mine}):
+                    of = [n for a, n in mine if a == at]
+                    build_rows(band_of(at), at, of[0], of[-1] + 1, tie)
+
+        columns(far, early, inner, 0, 3, True)
+        tie = for_sibling(0, 0, inner)
+        build_rows(band_of(3), 3, 0, tiles, tie)
+        for_sibling(1, 1, inner)
         edges()
-        var_copy().wait_recv()
-        for slot in range(chips - 1):
-            send_weight(slot)
-        columns(far, early, outer, 2, share)
-        for_sibling(0, 0)
-        for_sibling(1, 1)
-        sib_copy(0).start()
-        sib_copy(1).start()
-        for_own(0, 2)
-        for_own(1, 3)
-        columns(near, total - early, inner, 4, share)
+        merge_edges()
+        for_own(0, 2, inner)
+        for_own(1, 3, inner)
+        columns(far, early, outer, 4, 2)
+        for slot in range(2):
+            for_sibling(slot, slot, outer)
+        for slot in range(2):
+            for_own(slot, 2 + slot, outer)
+        for slot in range(2):
+            sib_copy(slot).start()
+        columns(near, total - early, inner, 6, 1)
+        columns(near, total - early, outer, 7, 1)
+        for_sibling(2, 4)
+        sib_copy(2).start()
         send_pair(0)
         send_pair(1)
-        columns(near, total - early, outer, 6, share)
-        for_sibling(2, 4)
-        sib_copy(2).start()
         for_own(2, 5)
         for_sibling(3, 6)
+        for_own(3, 7)
         sib_copy(3).start()
-        own_sums()
-        for slot in range(chips - 1):
-            add_weight(slot)
-        for_own(3, 7)
         send_pair(2)
     else:
         edges()
-
-        def one(p, carry):
-            build(2 * p)
-            build(2 * p + 1)
-            for k in range(blocks):
-                col_step(p, 0, height + 2 * LEAD, [k])
+        merge_edges()
+        for b in range(basis):
+            build(b)
+
+        def one(g, carry):
+            for p in range(steps):
+                for which in (inner, outer):
+                    col_step(p, pl.multiple_of(g * strip, 16), strip, which)
             return carry
 
-        lax.fori_loop(0, steps, one, 0)
-        var_copy().wait_recv()
-        each(0, chips - 1, send_weight)
+        lax.fori_loop(0, PACK, one, 0)
 
         def sibling_band(slot):
             for_sibling(slot)
@@ -449,19 +482,13 @@
         each(0, chips, sibling_band)
         each(0, chips, for_own)
         each(0, chips - 1, send_pair)
-        own_sums()
-        each(0, chips - 1, add_weight)
-
+
+    add_weights()
     add_own()
     each(0, chips - 1, add_pixels)
 
-    var_copy().wait_send()
-
-    def drain(slot):
-        w_copy(slot).wait_send()
-        pix_copy(slot).wait_send()
-
-    each(0, chips - 1, drain)
+    for_vars(lambda slot, other: var_copy(slot, other).wait_send())
+    each(0, chips - 1, lambda slot: pix_copy(slot).wait_send())
     each(0, chips, lambda slot: sib_copy(slot).wait_send())
 
     @pl.when(has_l)
@@ -503,28 +530,24 @@
             pltpu.VMEM((2, tall // PACK, LANES), bf16),
             pltpu.VMEM((tall, cols + LANES), bf16),
             pltpu.VMEM((CORES, chips, ROWS_DEV, cols), bf16),
-            pltpu.VMEM((chips, ROWS_DEV, cols), bf16),
-            pltpu.VMEM((chips, ROWS_DEV, cols), bf16),
-            pltpu.VMEM((chips, ROWS_DEV, cols), bf16),
+            pltpu.VMEM((chips, CORES, ROWS_DEV, cols), bf16),
             pltpu.VMEM((chips, ROWS_DEV, cols), f32),
             pltpu.VMEM((chips, ROWS_DEV, cols), f32),
             pltpu.VMEM((chips, ROWS_DEV, cols), f32),
             pltpu.VMEM((chips, ROWS_DEV, cols), bf16),
             pltpu.VMEM((chips, ROWS_DEV, cols), bf16),
-            pltpu.VMEM((24, 2 * LANES), f32),
+            pltpu.VMEM((24, LANES), f32),
             pltpu.VMEM((basis, LANES, 2 * LANES), bf16),
-            pltpu.VMEM((basis, height + 2 * TOP, cols), bf16),
+            [pltpu.VMEM((2, tall + 32, cols), bf16)] * (basis // 2),
             pltpu.VMEM((ROWS_DEV, deep), f32),
             pltpu.VMEM((8, deep), f32),
-            pltpu.VMEM((visits if few else 1, 2 * ROWS_DEV, deep), bf16),
+            [pltpu.VMEM((2 * ROWS_DEV, deep), bf16)] * (visits if few else 1),
             pltpu.VMEM((ROWS_DEV, deep), bf16),
             dma((7,)),
             dma((2,)),
             dma((2,)),
-            dma((1,)),
-            dma((1,)),
-            dma((chips,)),
-            dma((chips,)),
+            dma((chips, CORES)),
+            dma((chips, CORES)),
             dma((chips,)),
             dma((chips,)),
             dma((chips,)),

time: 20 us -> 18.2 us (0.910)
  Pallas kernels: 17.6 us -> 15.7 us
    pallas_call x1, Pallas kernels: 17.6 us -> 15.7 us  [per_device(): pl.pallas_call(functools.partial(kernel, visits, skies), out_shape=jax.Sh...]
where the time goes in v2:
time: 18.2 us; the launch traced here: 18 us
  Pallas kernels  15.7 us (86%)
  other arithmetic  1.62 us (9%)
  between operations  0.64 us (4%)
    pallas_call x1, Pallas kernels, per_device(): pl.pallas_call(functools.partial(kernel, visits, skies), out_shape=jax.Sh...  15.7 us
    div x1, other arithmetic, per_device(): return (sums[0] / jnp.maximum(sums[1], 1.0), sums[1])  1.62 us

profile of v2, /device:TPU:0, one launch (start us, length us, event | category | flops | bytes accessed | tf_op | source)
XLA Modules:
  0.0 18.0 jit_solution(327799350224477561)
XLA Ops:
  0.6 15.7 %shard_map.86 = f32[2,48,512]{2,1,0:T(8,128)} custom-call(bf16[1,384,512]{2,1,0:T(8,128)(2,1)} %image_hbm.1, bf16[1,384,512]{2,1,0:T(8,128)(2,1)} %var_hbm.1, s32[1,384,512]{2,1,0:T(8,128)} %bits_hbm.1, s32[1,4]{1,0:T(1,128)} %boxes_hbm.1, bf16[20,41]{1,0:T(8,128)(2,1)} %rowf_hbm.1, bf16[20,41]{1,0:T(8,128)(2,1)} %colf_hbm.1, f32[6,1,20]{2,1,0:T(1,128)} %bitcast.6), custom_call_target="tpu_custom_call" | custom-call | tf_op jit(solution)/shard_map/pallas_call | solution.py:516
  16.4 1.6 %bitcast_divide_fusion = (f32[48,512]{1,0:T(8,128)}, f32[48,512]{1,0:T(8,128)}) fusion(f32[2,48,512]{2,1,0:T(8,128)} %shard_map.86), kind=kLoop, calls=%fused_computation | loop fusion | flops 49152 | bytes 393216 | tf_op jit(solution)/shard_map/div | solution.py:560

commit v3 on v2

--- a/solution.py
+++ b/solution.py
@@ -15,6 +15,7 @@
 LEAD = 8
 TOP = 24
 WIN = 2 * ROWS_DEV
+UNITS = 2
 PACK = 5
 TERMS = 6
 MESH = pl.DeviceIdType.MESH
@@ -22,8 +23,8 @@
 
 def weight_of(plane):
     plane = plane.astype(jnp.float32)
-    positive = plane > 0
-    return jnp.where(positive, 1.0 / jnp.where(positive, plane, 1.0), 0.0)
+    near = pl.reciprocal(plane, approx=True)
+    return jnp.where(plane > 0, near * (2.0 - plane * near), 0.0)
 
 
 def kernel(
@@ -48,12 +49,16 @@
     edge_got,
     wide,
     masked,
-    got_var,
+    sib_var,
+    pair_w,
+    got_w,
     own_pix,
     sib_send,
     sib_pix,
     pair_pix,
     got_pix,
+    cross_pix,
+    got_cross,
     filt,
     col_mats,
     passed,
@@ -66,16 +71,21 @@
     halo_recv,
     var_send,
     var_recv,
+    w_send,
+    w_recv,
     sib_send_sem,
     sib_recv_sem,
     pix_send,
     pix_recv,
+    cross_send,
+    cross_recv,
 ):
     height, cols = var_ref.shape[1], var_ref.shape[2]
     width = cols * skies
     basis, taps = rowf_ref.shape
     blocks = cols // LANES
-    inner, outer = list(range(1, blocks - 1)), [0, blocks - 1]
+    inner, outer = units = list(range(1, blocks - 1)), [0, blocks - 1]
+    per_unit = blocks // UNITS
     chips = visits // CORES
     few = chips == 4
     deep = basis * WIN
@@ -229,37 +239,35 @@
     def peer(slot):
         return (chip_at(slot) * CORES + core, z)
 
-    def var_copy(slot, other):
-        side = 1 - core if other else core
+    def var_copy():
+        return remote(masked.at[1 - core], sib_var, var_send.at[0], var_recv.at[0], (sibling, z))
+
+    def w_copy(slot):
         return remote(
-            masked.at[side, chip_at(slot)],
-            got_var.at[slot, other],
-            var_send.at[slot, other],
-            var_recv.at[slot, other],
-            (chip_at(slot) * CORES + side, z),
-        )
-
-    def for_vars(act):
-        def both(slot):
-            act(slot, 0)
-            act(slot, 1)
-
-        each(0, chips - 1, both)
-        act(chips - 1, 1)
-
-    def sib_copy(slot):
+            pair_w.at[slot], got_w.at[slot], w_send.at[slot], w_recv.at[slot], peer(slot)
+        )
+
+    def sib_copy(unit, slot):
         return remote(
-            sib_send.at[slot],
-            sib_pix.at[slot],
-            sib_send_sem.at[slot],
-            sib_recv_sem.at[slot],
+            sib_send.at[unit, slot],
+            sib_pix.at[unit, slot],
+            sib_send_sem.at[unit, slot],
+            sib_recv_sem.at[unit, slot],
             (sibling, z),
         )
 
-    def pix_copy(slot):
+    def pix_copy(unit, slot):
         return remote(
-            pair_pix.at[slot], got_pix.at[slot], pix_send.at[slot], pix_recv.at[slot], peer(slot)
-        )
+            pair_pix.at[unit, slot],
+            got_pix.at[unit, slot],
+            pix_send.at[unit, slot],
+            pix_recv.at[unit, slot],
+            peer(slot),
+        )
+
+    def cross_copy():
+        target = (chip_at(2) * CORES + 1 - core, z)
+        return remote(cross_pix, got_cross, cross_send.at[0], cross_recv.at[0], target)
 
     pl.semaphore_wait(barrier, visits - 1 + has_l.astype(jnp.int32) + has_r.astype(jnp.int32))
 
@@ -290,7 +298,7 @@
         return carry
 
     lax.fori_loop(0, visits, mask_band, 0, unroll=few)
-    for_vars(lambda slot, other: var_copy(slot, other).start())
+    var_copy().start()
 
     def col_step(p, first, rows, which):
         parts = [wide[pl.ds(first, rows), k * LANES : (k + 2) * LANES] for k in which]
@@ -309,12 +317,8 @@
                 ].astype(bf16)
         return out[0:1, 0:LANES] * 0.0
 
-    def picked(plane, which):
-        if len(which) == blocks:
-            return plane
-        return jnp.concatenate([plane[..., k * LANES : (k + 1) * LANES] for k in which], axis=-1)
-
-    def weighted(slot, side, at, which):
+    def weighted(unit, slot, side, at):
+        which = units[unit]
         at_chip = chip_at(slot)
         band = at_chip * CORES + side
         if not few:
@@ -335,31 +339,36 @@
             axis=1,
         )
         out = jnp.dot(mats, lines, preferred_element_type=f32)
-        x = (2 * lax.broadcasted_iota(jnp.int32, (1, cols), 1) + 1 - cols).astype(f32) / width
-        x = picked(x, which)
+        x = jnp.concatenate(
+            [(2 * (k * LANES + lane) + 1 - cols).astype(f32) / width for k in which], axis=1
+        )
         pixels = out[0:ROWS_DEV] + x * (
             out[ROWS_DEV : 2 * ROWS_DEV] + x * out[2 * ROWS_DEV : 3 * ROWS_DEV]
         )
-        return pixels * weight_of(picked(masked[side, at_chip], which)), out[0:1, 0:LANES] * 0.0
-
-    def put(ref, slot, side, at, which):
-        result, tie = weighted(slot, side, at, which)
-        for n, k in enumerate(which):
-            ref[slot, :, k * LANES : (k + 1) * LANES] = result[:, n * LANES : (n + 1) * LANES]
+        plane = masked[side, at_chip]
+        plane = jnp.concatenate([plane[:, k * LANES : (k + 1) * LANES] for k in which], axis=1)
+        return pixels * weight_of(plane), out[0:1, 0:LANES] * 0.0
+
+    def for_sibling(unit, slot, at=0):
+        sib_send[unit, slot], tie = weighted(unit, slot, 1 - core, at)
         return tie
 
-    every_block = list(range(blocks))
-
-    def for_sibling(slot, at=0, which=every_block):
-        return put(sib_send, slot, 1 - core, at, which)
-
-    def for_own(slot, at=0, which=every_block):
-        return put(own_pix, slot, core, at, which)
-
-    def send_pair(slot):
-        sib_copy(slot).wait_recv()
-        pair_pix[slot] = (own_pix[slot] + sib_pix[slot]).astype(bf16)
-        pix_copy(slot).start()
+    def for_own(unit, slot, at=0):
+        own_pix[unit, slot], tie = weighted(unit, slot, core, at)
+        return tie
+
+    def send_pair(unit, slot):
+        sib_copy(unit, slot).wait_recv()
+        pair_pix[unit, slot] = (own_pix[unit, slot] + sib_pix[unit, slot]).astype(bf16)
+        pix_copy(unit, slot).start()
+
+    def pair_weight(slot):
+        at_chip = chip_at(slot)
+        return weight_of(masked[core, at_chip]) + weight_of(sib_var[at_chip])
+
+    def send_weight(slot):
+        pair_w[slot] = pair_weight(slot).astype(bf16)
+        w_copy(slot).start()
 
     def edges():
         @pl.when(has_l)
@@ -392,21 +401,35 @@
             ).astype(bf16)
 
     def add_weights():
-        sums_ref[1] = weight_of(masked[core, chip])
-
-        def one(slot, other):
-            var_copy(slot, other).wait_recv()
-            sums_ref[1] += weight_of(got_var[slot, other])
-
-        for_vars(one)
-
-    def add_own():
-        sib_copy(chips - 1).wait_recv()
-        sums_ref[0] = own_pix[chips - 1] + sib_pix[chips - 1]
-
-    def add_pixels(slot):
-        pix_copy(slot).wait_recv()
-        sums_ref[0] += got_pix[slot].astype(f32)
+        sums_ref[1] = pair_weight(chips - 1)
+
+        def one(slot):
+            w_copy(slot).wait_recv()
+            sums_ref[1] += got_w[slot].astype(f32)
+
+        each(0, chips - 1, one)
+
+    def in_place(plane_of):
+        lanes_of = {}
+        for unit, which in enumerate(units):
+            part = plane_of(unit)
+            for n, k in enumerate(which):
+                lanes_of[k] = part[:, n * LANES : (n + 1) * LANES]
+        return jnp.concatenate([lanes_of[k] for k in range(blocks)], axis=1)
+
+    def add_to(unit, value, first=False):
+        for n, k in enumerate(units[unit]):
+            lanes = slice(k * LANES, (k + 1) * LANES)
+            part = value[:, n * LANES : (n + 1) * LANES]
+            sums_ref[0, :, lanes] = part if first else sums_ref[0, :, lanes] + part
+
+    def add_own(unit):
+        sib_copy(unit, chips - 1).wait_recv()
+        add_to(unit, own_pix[unit, chips - 1] + sib_pix[unit, chips - 1], True)
+
+    def add_pixels(unit, slot):
+        pix_copy(unit, slot).wait_recv()
+        add_to(unit, got_pix[unit, slot].astype(f32))
 
     steps = basis // 2
     if few:
@@ -416,7 +439,7 @@
         early = half + 2 * LEAD + LEAD * 2
         far = pl.multiple_of((1 - group) * (total - early), 16)
         near = pl.multiple_of(group * early, 16)
-        bands = [(0, 1), (1, 1), (0, 0), (1, 0), (2, 1), (2, 0), (3, 1), (3, 0)]
+        bands = [(0, 1), (1, 1), (2, 1), (0, 0), (1, 0), (2, 0), (3, 1), (3, 0)]
 
         def band_of(at):
             slot, other = bands[at]
@@ -435,32 +458,47 @@
                     of = [n for a, n in mine if a == at]
                     build_rows(band_of(at), at, of[0], of[-1] + 1, tie)
 
-        columns(far, early, inner, 0, 3, True)
-        tie = for_sibling(0, 0, inner)
-        build_rows(band_of(3), 3, 0, tiles, tie)
-        for_sibling(1, 1, inner)
+        def rows_beside(at, tie):
+            build_rows(band_of(at), at, 0, tiles, tie)
+
+        columns(far, early, inner, 0, 2, True)
+        columns(near, total - early, inner, 2, 3)
+        rows_beside(5, for_sibling(0, 0, 0))
+        for_sibling(0, 1, 1)
+        for_sibling(0, 2, 2)
+        for_own(0, 0, 3)
+        var_copy().wait_recv()
+        for slot in range(3):
+            send_weight(slot)
+            sib_copy(0, slot).start()
+        tie = for_own(0, 1, 4)
+        rows_beside(6, tie)
+        rows_beside(7, tie)
+        for_own(0, 2, 5)
+        for_sibling(0, 3, 6)
+        for_own(0, 3, 7)
         edges()
+        sib_copy(0, 3).start()
         merge_edges()
-        for_own(0, 2, inner)
-        for_own(1, 3, inner)
-        columns(far, early, outer, 4, 2)
+        columns(far, early, outer, 0, 0)
         for slot in range(2):
-            for_sibling(slot, slot, outer)
+            for_sibling(1, slot, slot)
         for slot in range(2):
-            for_own(slot, 2 + slot, outer)
+            sib_copy(1, slot).start()
+        for slot in range(3):
+            send_pair(0, slot)
         for slot in range(2):
-            sib_copy(slot).start()
-        columns(near, total - early, inner, 6, 1)
-        columns(near, total - early, outer, 7, 1)
-        for_sibling(2, 4)
-        sib_copy(2).start()
-        send_pair(0)
-        send_pair(1)
-        for_own(2, 5)
-        for_sibling(3, 6)
-        for_own(3, 7)
-        sib_copy(3).start()
-        send_pair(2)
+            for_own(1, slot, 3 + slot)
+        columns(near, total - early, outer, 0, 0)
+        cross_pix[...] = weighted(1, 2, 1 - core, 2)[0].astype(bf16)
+        pair_pix[1, 2] = weighted(1, 2, core, 5)[0].astype(bf16)
+        for slot in range(2):
+            send_pair(1, slot)
+        cross_copy().start()
+        pix_copy(1, 2).start()
+        for_sibling(1, 3, 6)
+        for_own(1, 3, 7)
+        sib_copy(1, 3).start()
     else:
         edges()
         merge_edges()
@@ -469,27 +507,42 @@
 
         def one(g, carry):
             for p in range(steps):
-                for which in (inner, outer):
+                for which in units:
                     col_step(p, pl.multiple_of(g * strip, 16), strip, which)
             return carry
 
         lax.fori_loop(0, PACK, one, 0)
-
-        def sibling_band(slot):
-            for_sibling(slot)
-            sib_copy(slot).start()
-
-        each(0, chips, sibling_band)
-        each(0, chips, for_own)
-        each(0, chips - 1, send_pair)
+        var_copy().wait_recv()
+        each(0, chips - 1, send_weight)
+        for unit in range(UNITS):
+
+            def sibling_band(slot):
+                for_sibling(unit, slot)
+                sib_copy(unit, slot).start()
+
+            each(0, chips, sibling_band)
+            each(0, chips, lambda slot: for_own(unit, slot))
+            each(0, chips - 1, lambda slot: send_pair(unit, slot))
 
     add_weights()
-    add_own()
-    each(0, chips - 1, add_pixels)
-
-    for_vars(lambda slot, other: var_copy(slot, other).wait_send())
-    each(0, chips - 1, lambda slot: pix_copy(slot).wait_send())
-    each(0, chips, lambda slot: sib_copy(slot).wait_send())
+    add_own(0)
+    each(0, chips - 1, lambda slot: add_pixels(0, slot))
+    add_own(1)
+
+    var_copy().wait_send()
+
+    def drain(slot):
+        w_copy(slot).wait_send()
+        for unit in range(UNITS):
+            pix_copy(unit, slot).wait_send()
+
+    each(0, chips - 1, drain)
+    for unit in range(UNITS):
+        each(
+            0,
+            chips,
+            lambda slot: None if few and (unit, slot) == (1, 2) else sib_copy(unit, slot).wait_send(),
+        )
 
     @pl.when(has_l)
     def _():
@@ -498,6 +551,16 @@
     @pl.when(has_r)
     def _():
         edge_copy(1, z + 1).wait_send()
+
+    if few:
+        cross_copy().wait_send()
+        add_pixels(1, 2)
+        cross_copy().wait_recv()
+        add_to(1, got_cross[...].astype(f32))
+        add_pixels(1, 1)
+        add_pixels(1, 0)
+    else:
+        each(0, chips - 1, lambda slot: add_pixels(1, slot))
 
 
 def per_device(image, variance, mask_bits, boxes, row_filters, col_filters, coeffs):
@@ -507,6 +570,7 @@
     chips = visits // CORES
     few = chips == 4
     deep = basis * WIN
+    span = cols // UNITS
     unit = 16 * PACK
     tall = (height + 2 * LEAD + unit - 1) // unit * unit
     coeffs = jnp.transpose(coeffs, (2, 0, 1))
@@ -530,12 +594,16 @@
             pltpu.VMEM((2, tall // PACK, LANES), bf16),
             pltpu.VMEM((tall, cols + LANES), bf16),
             pltpu.VMEM((CORES, chips, ROWS_DEV, cols), bf16),
-            pltpu.VMEM((chips, CORES, ROWS_DEV, cols), bf16),
-            pltpu.VMEM((chips, ROWS_DEV, cols), f32),
-            pltpu.VMEM((chips, ROWS_DEV, cols), f32),
-            pltpu.VMEM((chips, ROWS_DEV, cols), f32),
             pltpu.VMEM((chips, ROWS_DEV, cols), bf16),
             pltpu.VMEM((chips, ROWS_DEV, cols), bf16),
+            pltpu.VMEM((chips, ROWS_DEV, cols), bf16),
+            pltpu.VMEM((UNITS, chips, ROWS_DEV, span), f32),
+            pltpu.VMEM((UNITS, chips, ROWS_DEV, span), f32),
+            pltpu.VMEM((UNITS, chips, ROWS_DEV, span), f32),
+            pltpu.VMEM((UNITS, chips, ROWS_DEV, span), bf16),
+            pltpu.VMEM((UNITS, chips, ROWS_DEV, span), bf16),
+            pltpu.VMEM((ROWS_DEV, span), bf16),
+            pltpu.VMEM((ROWS_DEV, span), bf16),
             pltpu.VMEM((24, LANES), f32),
             pltpu.VMEM((basis, LANES, 2 * LANES), bf16),
             [pltpu.VMEM((2, tall + 32, cols), bf16)] * (basis // 2),
@@ -546,12 +614,16 @@
             dma((7,)),
             dma((2,)),
             dma((2,)),
-            dma((chips, CORES)),
-            dma((chips, CORES)),
+            dma((1,)),
+            dma((1,)),
             dma((chips,)),
             dma((chips,)),
-            dma((chips,)),
-            dma((chips,)),
+            dma((UNITS, chips)),
+            dma((UNITS, chips)),
+            dma((UNITS, chips)),
+            dma((UNITS, chips)),
+            dma((1,)),
+            dma((1,)),
         ],
         compiler_params=pltpu.CompilerParams(
             collective_id=0, has_side_effects=True, vmem_limit_bytes=62 * 1024 * 1024

time: 18.2 us -> 17.4 us (0.956)
  Pallas kernels: 15.7 us -> 15 us
    pallas_call x1, Pallas kernels: 15.7 us -> 15 us  [per_device(): pl.pallas_call(functools.partial(kernel, visits, skies), out_shape=jax.Sh...]
where the time goes in v3:
time: 17.4 us; the launch traced here: 17.2 us
  Pallas kernels  15 us (86%)
  other arithmetic  1.62 us (9%)
  between operations  0.64 us (4%)
    pallas_call x1, Pallas kernels, per_device(): pl.pallas_call(functools.partial(kernel, visits, skies), out_shape=jax.Sh...  15 us
    div x1, other arithmetic, per_device(): return (sums[0] / jnp.maximum(sums[1], 1.0), sums[1])  1.62 us

profile of v3, /device:TPU:0, one launch (start us, length us, event | category | flops | bytes accessed | tf_op | source)
XLA Modules:
  0.0 17.2 jit_solution(12646779602262819252)
XLA Ops:
  0.6 15.0 %shard_map.86 = f32[2,48,512]{2,1,0:T(8,128)} custom-call(bf16[1,384,512]{2,1,0:T(8,128)(2,1)} %image_hbm.1, bf16[1,384,512]{2,1,0:T(8,128)(2,1)} %var_hbm.1, s32[1,384,512]{2,1,0:T(8,128)} %bits_hbm.1, s32[1,4]{1,0:T(1,128)} %boxes_hbm.1, bf16[20,41]{1,0:T(8,128)(2,1)} %rowf_hbm.1, bf16[20,41]{1,0:T(8,128)(2,1)} %colf_hbm.1, f32[6,1,20]{2,1,0:T(1,128)} %bitcast.6), custom_call_target="tpu_custom_call" | custom-call | tf_op jit(solution)/shard_map/pallas_call | solution.py:580
  15.6 1.6 %bitcast_divide_fusion = (f32[48,512]{1,0:T(8,128)}, f32[48,512]{1,0:T(8,128)}) fusion(f32[2,48,512]{2,1,0:T(8,128)} %shard_map.86), kind=kLoop, calls=%fused_computation | loop fusion | flops 49152 | bytes 393216 | tf_op jit(solution)/shard_map/div | solution.py:632

commit v4 on v3

--- a/solution.py
+++ b/solution.py
@@ -49,9 +49,7 @@
     edge_got,
     wide,
     masked,
-    sib_var,
-    pair_w,
-    got_w,
+    got_var,
     own_pix,
     sib_send,
     sib_pix,
@@ -71,8 +69,6 @@
     halo_recv,
     var_send,
     var_recv,
-    w_send,
-    w_recv,
     sib_send_sem,
     sib_recv_sem,
     pix_send,
@@ -239,13 +235,23 @@
     def peer(slot):
         return (chip_at(slot) * CORES + core, z)
 
-    def var_copy():
-        return remote(masked.at[1 - core], sib_var, var_send.at[0], var_recv.at[0], (sibling, z))
-
-    def w_copy(slot):
+    def var_copy(slot, other):
+        side = 1 - core if other else core
         return remote(
-            pair_w.at[slot], got_w.at[slot], w_send.at[slot], w_recv.at[slot], peer(slot)
-        )
+            masked.at[side, chip_at(slot)],
+            got_var.at[slot, other],
+            var_send.at[slot, other],
+            var_recv.at[slot, other],
+            (chip_at(slot) * CORES + side, z),
+        )
+
+    def for_vars(act):
+        def both(slot):
+            act(slot, 0)
+            act(slot, 1)
+
+        each(0, chips - 1, both)
+        act(chips - 1, 1)
 
     def sib_copy(unit, slot):
         return remote(
@@ -282,23 +288,24 @@
     for load in loads[4:]:
         load.wait()
     box = [boxes_ref[0, i] for i in range(4)]
-    col_index = col_first + lax.broadcasted_iota(jnp.int32, (ROWS_DEV, cols), 1)
-    col_inside = (col_index >= box[2]) & (col_index < box[3])
-    row_iota = lax.broadcasted_iota(jnp.int32, (ROWS_DEV, cols), 0)
+    col_index = col_first + lax.broadcasted_iota(jnp.int32, (1, cols), 1)
+    col_out = jnp.where((col_index >= box[2]) & (col_index < box[3]), 0, 1)
+    row_iota = lax.broadcasted_iota(jnp.int32, (ROWS_DEV, LANES), 0)
 
     def mask_band(band, carry):
         first = pl.multiple_of(band * ROWS_DEV, ROWS_DEV)
         rows = pl.ds(first, ROWS_DEV)
         row_index = first + row_iota
-        inside = (row_index >= box[0]) & (row_index < box[1]) & col_inside
-        inside = inside & ((bits_ref[0, rows, :] & REJECT) == 0)
+        row_out = jnp.where((row_index >= box[0]) & (row_index < box[1]), 0, 1)
+        row_out = jnp.concatenate([row_out] * blocks, axis=1)
+        out = (bits_ref[0, rows, :] & REJECT) | row_out | col_out
         masked[lax.rem(band, CORES), band // CORES] = jnp.where(
-            inside, var_ref[0, rows, :].astype(f32), 0.0
+            out == 0, var_ref[0, rows, :].astype(f32), 0.0
         ).astype(bf16)
         return carry
 
     lax.fori_loop(0, visits, mask_band, 0, unroll=few)
-    var_copy().start()
+    for_vars(lambda slot, other: var_copy(slot, other).start())
 
     def col_step(p, first, rows, which):
         parts = [wide[pl.ds(first, rows), k * LANES : (k + 2) * LANES] for k in which]
@@ -362,14 +369,6 @@
         pair_pix[unit, slot] = (own_pix[unit, slot] + sib_pix[unit, slot]).astype(bf16)
         pix_copy(unit, slot).start()
 
-    def pair_weight(slot):
-        at_chip = chip_at(slot)
-        return weight_of(masked[core, at_chip]) + weight_of(sib_var[at_chip])
-
-    def send_weight(slot):
-        pair_w[slot] = pair_weight(slot).astype(bf16)
-        w_copy(slot).start()
-
     def edges():
         @pl.when(has_l)
         def _():
@@ -401,13 +400,13 @@
             ).astype(bf16)
 
     def add_weights():
-        sums_ref[1] = pair_weight(chips - 1)
-
-        def one(slot):
-            w_copy(slot).wait_recv()
-            sums_ref[1] += got_w[slot].astype(f32)
-
-        each(0, chips - 1, one)
+        sums_ref[1] = weight_of(masked[core, chip])
+
+        def one(slot, other):
+            var_copy(slot, other).wait_recv()
+            sums_ref[1] += weight_of(got_var[slot, other])
+
+        for_vars(one)
 
     def in_place(plane_of):
         lanes_of = {}
@@ -467,18 +466,13 @@
         for_sibling(0, 1, 1)
         for_sibling(0, 2, 2)
         for_own(0, 0, 3)
-        var_copy().wait_recv()
-        for slot in range(3):
-            send_weight(slot)
-            sib_copy(0, slot).start()
         tie = for_own(0, 1, 4)
         rows_beside(6, tie)
         rows_beside(7, tie)
         for_own(0, 2, 5)
-        for_sibling(0, 3, 6)
-        for_own(0, 3, 7)
         edges()
-        sib_copy(0, 3).start()
+        for slot in range(3):
+            sib_copy(0, slot).start()
         merge_edges()
         columns(far, early, outer, 0, 0)
         for slot in range(2):
@@ -489,11 +483,14 @@
             send_pair(0, slot)
         for slot in range(2):
             for_own(1, slot, 3 + slot)
+        for_sibling(0, 3, 6)
+        for_own(0, 3, 7)
+        for slot in range(2):
+            send_pair(1, slot)
+        sib_copy(0, 3).start()
         columns(near, total - early, outer, 0, 0)
         cross_pix[...] = weighted(1, 2, 1 - core, 2)[0].astype(bf16)
         pair_pix[1, 2] = weighted(1, 2, core, 5)[0].astype(bf16)
-        for slot in range(2):
-            send_pair(1, slot)
         cross_copy().start()
         pix_copy(1, 2).start()
         for_sibling(1, 3, 6)
@@ -512,8 +509,6 @@
             return carry
 
         lax.fori_loop(0, PACK, one, 0)
-        var_copy().wait_recv()
-        each(0, chips - 1, send_weight)
         for unit in range(UNITS):
 
             def sibling_band(slot):
@@ -529,10 +524,9 @@
     each(0, chips - 1, lambda slot: add_pixels(0, slot))
     add_own(1)
 
-    var_copy().wait_send()
+    for_vars(lambda slot, other: var_copy(slot, other).wait_send())
 
     def drain(slot):
-        w_copy(slot).wait_send()
         for unit in range(UNITS):
             pix_copy(unit, slot).wait_send()
 
@@ -594,9 +588,7 @@
             pltpu.VMEM((2, tall // PACK, LANES), bf16),
             pltpu.VMEM((tall, cols + LANES), bf16),
             pltpu.VMEM((CORES, chips, ROWS_DEV, cols), bf16),
-            pltpu.VMEM((chips, ROWS_DEV, cols), bf16),
-            pltpu.VMEM((chips, ROWS_DEV, cols), bf16),
-            pltpu.VMEM((chips, ROWS_DEV, cols), bf16),
+            pltpu.VMEM((chips, CORES, ROWS_DEV, cols), bf16),
             pltpu.VMEM((UNITS, chips, ROWS_DEV, span), f32),
             pltpu.VMEM((UNITS, chips, ROWS_DEV, span), f32),
             pltpu.VMEM((UNITS, chips, ROWS_DEV, span), f32),
@@ -614,10 +606,8 @@
             dma((7,)),
             dma((2,)),
             dma((2,)),
-            dma((1,)),
-            dma((1,)),
-            dma((chips,)),
-            dma((chips,)),
+            dma((chips, CORES)),
+            dma((chips, CORES)),
             dma((UNITS, chips)),
             dma((UNITS, chips)),
             dma((UNITS, chips)),

time: 17.4 us -> 17 us (0.977)
  Pallas kernels: 15 us -> 14.6 us
    pallas_call x1, Pallas kernels: 15 us -> 14.6 us  [per_device(): pl.pallas_call(functools.partial(kernel, visits, skies), out_shape=jax.Sh...]
where the time goes in v4:
time: 17 us; the launch traced here: 16.8 us
  Pallas kernels  14.6 us (86%)
  other arithmetic  1.62 us (10%)
  between operations  0.64 us (4%)
    pallas_call x1, Pallas kernels, per_device(): pl.pallas_call(functools.partial(kernel, visits, skies), out_shape=jax.Sh...  14.6 us
    div x1, other arithmetic, per_device(): return (sums[0] / jnp.maximum(sums[1], 1.0), sums[1])  1.62 us

profile of v4, /device:TPU:0, one launch (start us, length us, event | category | flops | bytes accessed | tf_op | source)
XLA Modules:
  0.0 16.8 jit_solution(4094869150312580959)
XLA Ops:
  0.6 14.6 %shard_map.86 = f32[2,48,512]{2,1,0:T(8,128)} custom-call(bf16[1,384,512]{2,1,0:T(8,128)(2,1)} %image_hbm.1, bf16[1,384,512]{2,1,0:T(8,128)(2,1)} %var_hbm.1, s32[1,384,512]{2,1,0:T(8,128)} %bits_hbm.1, s32[1,4]{1,0:T(1,128)} %boxes_hbm.1, bf16[20,41]{1,0:T(8,128)(2,1)} %rowf_hbm.1, bf16[20,41]{1,0:T(8,128)(2,1)} %colf_hbm.1, f32[6,1,20]{2,1,0:T(1,128)} %bitcast.6), custom_call_target="tpu_custom_call" | custom-call | tf_op jit(solution)/shard_map/pallas_call | solution.py:574
  15.2 1.6 %bitcast_divide_fusion = (f32[48,512]{1,0:T(8,128)}, f32[48,512]{1,0:T(8,128)}) fusion(f32[2,48,512]{2,1,0:T(8,128)} %shard_map.86), kind=kLoop, calls=%fused_computation | loop fusion | flops 49152 | bytes 393216 | tf_op jit(solution)/shard_map/div | solution.py:622

commit v5 on v4

--- a/solution.py
+++ b/solution.py
@@ -111,20 +111,6 @@
 
             lax.fori_loop(first, last, one, 0)
 
-    barrier = pltpu.get_barrier_semaphore()
-    for step in range(1, visits):
-        pl.semaphore_signal(
-            barrier, inc=1, device_id=(lax.rem(v + step, visits), z), device_id_type=MESH
-        )
-
-    @pl.when(has_l)
-    def _():
-        pl.semaphore_signal(barrier, inc=1, device_id=(v, z - 1), device_id_type=MESH)
-
-    @pl.when(has_r)
-    def _():
-        pl.semaphore_signal(barrier, inc=1, device_id=(v, z + 1), device_id_type=MESH)
-
     pairs = (
         (rowf_hbm, rowf_ref),
         (colf_hbm, colf_ref),
@@ -140,14 +126,29 @@
     for load in loads:
         load.start()
 
+    barrier = pltpu.get_barrier_semaphore()
+    for step in range(1, visits):
+        pl.semaphore_signal(
+            barrier, inc=1, device_id=(lax.rem(v + step, visits), z), device_id_type=MESH
+        )
+
+    @pl.when(has_l)
+    def _():
+        pl.semaphore_signal(barrier, inc=1, device_id=(v, z - 1), device_id_type=MESH)
+
+    @pl.when(has_r)
+    def _():
+        pl.semaphore_signal(barrier, inc=1, device_id=(v, z + 1), device_id_type=MESH)
+
     below = image_ref.shape[0] - 16 - height
     image_ref[0:16, :] = jnp.zeros((16, cols), bf16)
     image_ref[16 + height :, :] = jnp.zeros((below, cols), bf16)
     col_first = z * cols
     for pair in passed:
         for h in range(2):
-            pair[h, 0:16, :] = jnp.zeros((16, cols), bf16)
-            pair[h, pair.shape[1] - 16 :, :] = jnp.zeros((16, cols), bf16)
+            for k in range(blocks):
+                pair[h, k, 0:16, :] = jnp.zeros((16, LANES), bf16)
+                pair[h, k, pair.shape[2] - 16 :, :] = jnp.zeros((16, LANES), bf16)
 
     for load in loads[:3]:
         load.wait()
@@ -161,8 +162,8 @@
     def build(b):
         col = jnp.broadcast_to(filt[pl.ds(b, 1), :], (LANES, LANES))
         col = pltpu.roll(col, 0, 1, stride=1, stride_axis=0)
-        col_mats[b, :, 0:LANES] = jnp.where(ahead, col, 0.0).astype(bf16)
-        col_mats[b, :, LANES : 2 * LANES] = jnp.where(ahead, 0.0, col).astype(bf16)
+        col_mats[0, b] = jnp.where(ahead, col, 0.0).astype(bf16)
+        col_mats[1, b] = jnp.where(ahead, 0.0, col).astype(bf16)
 
     group_of = lax.broadcasted_iota(jnp.int32, (1, deep), 1) // WIN
     tap_of = lax.broadcasted_iota(jnp.int32, (1, deep), 1) - group_of * WIN - (TOP - RAD)
@@ -183,7 +184,9 @@
     factors[2:3] = c[5]
     factors[3:4] = c[1] + (2.0 * xc) * c[3]
     factors[4:5] = c[4]
-    row_last[...] = (toeplitz[...] * c[3]).astype(bf16)
+    last = (toeplitz[...] * c[3]).astype(bf16)
+    for n in range(deep // LANES):
+        row_last[n] = last[:, n * LANES : (n + 1) * LANES]
     y_iota = lax.broadcasted_iota(jnp.int32, (ROWS_DEV, LANES), 0)
     tiles = deep // LANES
 
@@ -193,19 +196,21 @@
             lanes = slice(n * LANES, (n + 1) * LANES)
             base = toeplitz[:, lanes]
             f = [factors[t : t + 1, lanes] for t in range(5)]
-            row_mats[at][0:ROWS_DEV, lanes] = (base * (f[0] + y * (f[1] + y * f[2]))).astype(bf16)
-            row_mats[at][ROWS_DEV : 2 * ROWS_DEV, lanes] = (base * (f[3] + y * f[4])).astype(bf16)
-
-    strip = wide.shape[0] // PACK
+            row_mats[at][n, 0:ROWS_DEV, :] = (base * (f[0] + y * (f[1] + y * f[2]))).astype(bf16)
+            row_mats[at][n, ROWS_DEV : 2 * ROWS_DEV, :] = (base * (f[3] + y * f[4])).astype(bf16)
+
+    strip = wide.shape[1] // PACK
     loads[3].wait()
     to_l = to_r = jnp.zeros((strip, LANES), f32)
     for g in range(PACK):
         rows = slice(g * strip, (g + 1) * strip)
-        part = image_ref[g * strip : (g + 1) * strip + 16, :].astype(f32)[LEAD : LEAD + strip]
-        part = pltpu.roll(part, RAD, 1)
-        wide[rows, LANES:cols] = part[:, LANES:].astype(bf16)
-        edge = part[:, :LANES]
-        wide[rows, cols:] = edge.astype(bf16)
+        ends = [
+            image_ref[g * strip : (g + 1) * strip + 16, k * LANES : (k + 1) * LANES].astype(f32)
+            for k in (blocks - 1, 0)
+        ]
+        edge = jnp.concatenate([end[LEAD : LEAD + strip] for end in ends], axis=1)
+        edge = pltpu.roll(edge, RAD, 1)[:, LANES:]
+        wide[blocks, rows, :] = edge.astype(bf16)
         at = g * RAD
         edge = pltpu.roll(edge, at, 1) if g else edge
         to_r = jnp.where((lane >= at) & (lane < at + RAD), edge, to_r)
@@ -284,6 +289,12 @@
     @pl.when(has_r)
     def _():
         edge_copy(1, z + 1).start()
+
+    for g in range(PACK):
+        part = image_ref[g * strip : (g + 1) * strip + 16, :].astype(f32)[LEAD : LEAD + strip]
+        part = pltpu.roll(part, RAD, 1)
+        for k in range(1, blocks):
+            wide[k, g * strip : (g + 1) * strip, :] = part[:, k * LANES : (k + 1) * LANES].astype(bf16)
 
     for load in loads[4:]:
         load.wait()
@@ -308,8 +319,13 @@
     for_vars(lambda slot, other: var_copy(slot, other).start())
 
     def col_step(p, first, rows, which):
-        parts = [wide[pl.ds(first, rows), k * LANES : (k + 2) * LANES] for k in which]
-        mats = col_mats[pl.ds(2 * p, 2)].reshape(2 * LANES, 2 * LANES)
+        parts = [
+            jnp.concatenate([wide[k + n, pl.ds(first, rows), :] for n in range(2)], axis=1)
+            for k in which
+        ]
+        mats = jnp.concatenate(
+            [col_mats[n, pl.ds(2 * p, 2)].reshape(2 * LANES, LANES) for n in range(2)], axis=1
+        )
         out = lax.dot_general(
             jnp.concatenate(parts, axis=0),
             mats,
@@ -319,7 +335,7 @@
         into = pl.ds(pl.multiple_of(first + 16, 16), rows)
         for n, k in enumerate(which):
             for h in range(2):
-                passed[p][h, into, k * LANES : (k + 1) * LANES] = out[
+                passed[p][h, k, into, :] = out[
                     n * rows : (n + 1) * rows, h * LANES : (h + 1) * LANES
                 ].astype(bf16)
         return out[0:1, 0:LANES] * 0.0
@@ -331,12 +347,14 @@
         if not few:
             build_rows(band, at, 0, tiles, 0.0)
         rows = pl.ds(pl.multiple_of(band * ROWS_DEV, 16), WIN)
-        mats = jnp.concatenate([row_mats[at][...], row_last[...]], axis=0)
+        mats = jnp.concatenate(
+            [jnp.concatenate([row_mats[at][n], row_last[n]], axis=0) for n in range(tiles)], axis=1
+        )
         lines = jnp.concatenate(
             [
                 jnp.concatenate(
                     [
-                        pair[:, rows, k * LANES : (k + 1) * LANES].reshape(2 * WIN, LANES)
+                        pair[:, k, rows, :].reshape(2 * WIN, LANES)
                         for pair in passed
                     ],
                     axis=0,
@@ -389,13 +407,13 @@
     def merge_edges():
         for g in range(PACK):
             rows = slice(g * strip, (g + 1) * strip)
-            mine = wide[rows, cols:].astype(f32)
+            mine = wide[blocks, rows, :].astype(f32)
             from_r, from_l = (edge_got[side].astype(f32) for side in range(2))
             if g:
                 from_r = pltpu.roll(from_r, LANES - g * RAD, 1)
                 from_l = pltpu.roll(from_l, LANES - g * RAD, 1)
-            wide[rows, 0:LANES] = jnp.where(lane < RAD, from_l, mine).astype(bf16)
-            wide[rows, cols:] = jnp.where(
+            wide[0, rows, :] = jnp.where(lane < RAD, from_l, mine).astype(bf16)
+            wide[blocks, rows, :] = jnp.where(
                 (lane >= RAD) & (lane < 2 * RAD), from_r, mine
             ).astype(bf16)
 
@@ -444,10 +462,10 @@
             slot, other = bands[at]
             return chip_at(slot) * CORES + (1 - core if other else core)
 
-        def columns(first, rows, which, base, count, build_too=False):
+        def columns(first, rows, which, base, count, build_too=False, some=range(steps)):
             pieces = [(base + n // tiles, n % tiles) for n in range(count * tiles)]
             each_step = -(-len(pieces) // steps)
-            for p in range(steps):
+            for p in some:
                 if build_too:
                     build(2 * p)
                     build(2 * p + 1)
@@ -483,19 +501,19 @@
             send_pair(0, slot)
         for slot in range(2):
             for_own(1, slot, 3 + slot)
-        for_sibling(0, 3, 6)
-        for_own(0, 3, 7)
+        columns(near, total - early, outer, 0, 0, some=range(steps // 2))
         for slot in range(2):
             send_pair(1, slot)
-        sib_copy(0, 3).start()
-        columns(near, total - early, outer, 0, 0)
+        columns(near, total - early, outer, 0, 0, some=range(steps // 2, steps))
         cross_pix[...] = weighted(1, 2, 1 - core, 2)[0].astype(bf16)
         pair_pix[1, 2] = weighted(1, 2, core, 5)[0].astype(bf16)
         cross_copy().start()
         pix_copy(1, 2).start()
-        for_sibling(1, 3, 6)
-        for_own(1, 3, 7)
-        sib_copy(1, 3).start()
+        for unit in range(UNITS):
+            for_sibling(unit, 3, 6)
+            for_own(unit, 3, 7)
+        for unit in range(UNITS):
+            sib_copy(unit, 3).start()
     else:
         edges()
         merge_edges()
@@ -586,7 +604,7 @@
             pltpu.VMEM(coeffs.shape, f32),
             pltpu.VMEM((2, tall // PACK, LANES), bf16),
             pltpu.VMEM((2, tall // PACK, LANES), bf16),
-            pltpu.VMEM((tall, cols + LANES), bf16),
+            pltpu.VMEM((cols // LANES + 1, tall, LANES), bf16),
             pltpu.VMEM((CORES, chips, ROWS_DEV, cols), bf16),
             pltpu.VMEM((chips, CORES, ROWS_DEV, cols), bf16),
             pltpu.VMEM((UNITS, chips, ROWS_DEV, span), f32),
@@ -597,12 +615,12 @@
             pltpu.VMEM((ROWS_DEV, span), bf16),
             pltpu.VMEM((ROWS_DEV, span), bf16),
             pltpu.VMEM((24, LANES), f32),
-            pltpu.VMEM((basis, LANES, 2 * LANES), bf16),
-            [pltpu.VMEM((2, tall + 32, cols), bf16)] * (basis // 2),
+            pltpu.VMEM((2, basis, LANES, LANES), bf16),
+            [pltpu.VMEM((2, cols // LANES, tall + 32, LANES), bf16)] * (basis // 2),
             pltpu.VMEM((ROWS_DEV, deep), f32),
             pltpu.VMEM((8, deep), f32),
-            [pltpu.VMEM((2 * ROWS_DEV, deep), bf16)] * (visits if few else 1),
-            pltpu.VMEM((ROWS_DEV, deep), bf16),
+            [pltpu.VMEM((deep // LANES, 2 * ROWS_DEV, LANES), bf16)] * (visits if few else 1),
+            pltpu.VMEM((deep // LANES, ROWS_DEV, LANES), bf16),
             dma((7,)),
             dma((2,)),
             dma((2,)),

time: 17 us -> 16.9 us (level)
  Pallas kernels: 14.6 us -> 14.4 us
where the time goes in v5:
time: 16.9 us; the launch traced here: 16.7 us
  Pallas kernels  14.4 us (85%)
  other arithmetic  1.62 us (10%)
  between operations  0.64 us (4%)
    pallas_call x1, Pallas kernels, per_device(): pl.pallas_call(functools.partial(kernel, visits, skies), out_shape=jax.Sh...  14.4 us
    div x1, other arithmetic, per_device(): return (sums[0] / jnp.maximum(sums[1], 1.0), sums[1])  1.62 us

profile of v5, /device:TPU:0, one launch (start us, length us, event | category | flops | bytes accessed | tf_op | source)
XLA Modules:
  0.0 16.7 jit_solution(13315546764963328482)
XLA Ops:
  0.6 14.4 %shard_map.86 = f32[2,48,512]{2,1,0:T(8,128)} custom-call(bf16[1,384,512]{2,1,0:T(8,128)(2,1)} %image_hbm.1, bf16[1,384,512]{2,1,0:T(8,128)(2,1)} %var_hbm.1, s32[1,384,512]{2,1,0:T(8,128)} %bits_hbm.1, s32[1,4]{1,0:T(1,128)} %boxes_hbm.1, bf16[20,41]{1,0:T(8,128)(2,1)} %rowf_hbm.1, bf16[20,41]{1,0:T(8,128)(2,1)} %colf_hbm.1, f32[6,1,20]{2,1,0:T(1,128)} %bitcast.6), custom_call_target="tpu_custom_call" | custom-call | tf_op jit(solution)/shard_map/pallas_call | solution.py:592
  15.1 1.6 %bitcast_divide_fusion = (f32[48,512]{1,0:T(8,128)}, f32[48,512]{1,0:T(8,128)}) fusion(f32[2,48,512]{2,1,0:T(8,128)} %shard_map.86), kind=kLoop, calls=%fused_computation | loop fusion | flops 49152 | bytes 393216 | tf_op jit(solution)/shard_map/div | solution.py:640

commit v6 on v5

--- a/solution.py
+++ b/solution.py
@@ -462,10 +462,10 @@
             slot, other = bands[at]
             return chip_at(slot) * CORES + (1 - core if other else core)
 
-        def columns(first, rows, which, base, count, build_too=False, some=range(steps)):
+        def columns(first, rows, which, base, count, build_too=False):
             pieces = [(base + n // tiles, n % tiles) for n in range(count * tiles)]
             each_step = -(-len(pieces) // steps)
-            for p in some:
+            for p in range(steps):
                 if build_too:
                     build(2 * p)
                     build(2 * p + 1)
@@ -501,10 +501,9 @@
             send_pair(0, slot)
         for slot in range(2):
             for_own(1, slot, 3 + slot)
-        columns(near, total - early, outer, 0, 0, some=range(steps // 2))
+        columns(near, total - early, outer, 0, 0)
         for slot in range(2):
             send_pair(1, slot)
-        columns(near, total - early, outer, 0, 0, some=range(steps // 2, steps))
         cross_pix[...] = weighted(1, 2, 1 - core, 2)[0].astype(bf16)
         pair_pix[1, 2] = weighted(1, 2, core, 5)[0].astype(bf16)
         cross_copy().start()

time: 16.9 us -> 16.9 us (level)
  no operation moved by 1% of the time
where the time goes in v6:
time: 16.9 us; the launch traced here: 16.7 us
  Pallas kernels  14.4 us (85%)
  other arithmetic  1.62 us (10%)
  between operations  0.64 us (4%)
    pallas_call x1, Pallas kernels, per_device(): pl.pallas_call(functools.partial(kernel, visits, skies), out_shape=jax.Sh...  14.4 us
    div x1, other arithmetic, per_device(): return (sums[0] / jnp.maximum(sums[1], 1.0), sums[1])  1.62 us

profile of v6, /device:TPU:0, one launch (start us, length us, event | category | flops | bytes accessed | tf_op | source)
XLA Modules:
  0.0 16.7 jit_solution(692937851251815392)
XLA Ops:
  0.6 14.4 %shard_map.86 = f32[2,48,512]{2,1,0:T(8,128)} custom-call(bf16[1,384,512]{2,1,0:T(8,128)(2,1)} %image_hbm.1, bf16[1,384,512]{2,1,0:T(8,128)(2,1)} %var_hbm.1, s32[1,384,512]{2,1,0:T(8,128)} %bits_hbm.1, s32[1,4]{1,0:T(1,128)} %boxes_hbm.1, bf16[20,41]{1,0:T(8,128)(2,1)} %rowf_hbm.1, bf16[20,41]{1,0:T(8,128)(2,1)} %colf_hbm.1, f32[6,1,20]{2,1,0:T(1,128)} %bitcast.6), custom_call_target="tpu_custom_call" | custom-call | tf_op jit(solution)/shard_map/pallas_call | solution.py:591
  15.0 1.6 %bitcast_divide_fusion = (f32[48,512]{1,0:T(8,128)}, f32[48,512]{1,0:T(8,128)}) fusion(f32[2,48,512]{2,1,0:T(8,128)} %shard_map.86), kind=kLoop, calls=%fused_computation | loop fusion | flops 49152 | bytes 393216 | tf_op jit(solution)/shard_map/div | solution.py:639
